TPU v7x, 128 devices: a whole 4x4x4 slice. The times are simulated.
128 devices in a mesh: span: 32 (over z, x, core), chord: 4 (over y).
Axes of the slice: x: 4, y: 4, z: 4, core: 2. Of those that a mesh axis runs over, the one named last changes fastest.
Arguments:
- surface_adjoint: bfloat16 [128, 2048, 2, 384], P('chord', 'span'), may hold values from -6 to 6
- velocity_adjoint: bfloat16 [2, 128, 2048, 2, 384], P(None, 'chord', 'span'), may hold values from -6 to 6
- metric: float32 [2, 128, 2048], P(None, 'chord', 'span'), may hold values from 0.5 to 2
- aic_blocks: bfloat16 [16, 128, 8, 2, 128, 128], P('chord', 'span'), may hold values from -0.125 to 0.125
- block_codes: int32 [16, 128, 8], P('chord', 'span'), may hold values from 0 to 8, all different within a row
- wake_adjoint: bfloat16 [65536, 2, 384], P(('span', 'chord')), may hold values from -3 to 3
- wake_owner: int32 [65536, 1], P(('span', 'chord')), may hold values from 0 to 31; in each aligned block of 512 rows (0 to 511, 512 to 1023, ...) at most 32 rows name the same one
- shed_station: int32 [65536], P(('span', 'chord')), may hold values from 0 to 63
Outputs:
- surface_out: bfloat16 [128, 2048, 2, 384], P('chord', 'span')
Inputs may be any that keep to these rules, and one draw needn't show every extreme that they name: `block_codes`: the 8 codes of one block are distinct. `wake_owner`: among the wake panels of one device no span index is named more than 32 times, and in some device one span index is named exactly 32 times.
All inputs are finite; a program needn't handle non-finite values.
Results may differ from a plain program's by a relative error of at most 0.0041.
Values may be sent and summed in bfloat16 or wider, within the bound.
No kernel may reach another device: no remote copies, remote signals or barrier semaphores. Data moves between devices by JAX's collectives and lax.ppermute only.
A program may use at most 256 MiB of HBM per device.

v0:
```python
import jax
import jax.numpy as jnp
from jax import lax
from jax.experimental import pallas as pl
from jax.experimental.pallas import tpu as pltpu
from jax.sharding import PartitionSpec as P

BC = 8
BS = 16
R = 384
CAP = 32
LANES = 128
META = 192
ROWS = 208
F32 = jnp.float32
BF16 = jnp.bfloat16


def split_parts(array):
    return jnp.swapaxes(array, -3, -2)


def shift(array, axis, step):
    count = lax.axis_size(axis)
    pairs = [(i, i + step) for i in range(count) if 0 <= i + step < count]
    return lax.ppermute(array, axis, pairs)


def pack_kernel(owner_ref, station_ref, wake_ref, out_ref):
    rows = owner_ref.shape[1]
    owners = out_ref.shape[0]
    owner = owner_ref[...]
    station = station_ref[...]
    named = lax.broadcasted_iota(jnp.int32, (owners, rows), 0) == owner
    hot = jnp.where(named, 1.0, 0.0).astype(F32)
    before = jnp.where(
        lax.broadcasted_iota(jnp.int32, (rows, rows), 0)
        < lax.broadcasted_iota(jnp.int32, (rows, rows), 1),
        1.0,
        0.0,
    ).astype(BF16)
    counts = jnp.dot(hot.astype(BF16), before, preferred_element_type=F32)
    rank = jnp.sum(hot * counts, axis=0, keepdims=True).astype(jnp.int32)
    slot = owner * CAP + rank
    stations = jnp.where(named, (station + 1).astype(F32), 0.0).astype(BF16)
    ranks = jnp.where(
        lax.broadcasted_iota(jnp.int32, (LANES, rows), 0) == rank, 1.0, 0.0
    ).astype(BF16)
    meta = lax.dot_general(
        stations, ranks, (((1,), (1,)), ((), ())), preferred_element_type=F32
    ).astype(BF16)
    for d in range(owners):
        out_ref[d, META:ROWS, :] = jnp.broadcast_to(meta[d : d + 1], (ROWS - META, LANES))
    values = jnp.concatenate([wake_ref[0], wake_ref[1]], axis=1)
    chunk = 256
    for first in range(0, owners * CAP, chunk):
        place = jnp.where(
            lax.broadcasted_iota(jnp.int32, (chunk, rows), 0) + first == slot, 1.0, 0.0
        ).astype(BF16)
        packed = jnp.dot(place, values, preferred_element_type=F32).astype(BF16)
        for d in range(chunk // CAP):
            for part in range(6):
                out_ref[first // CAP + d, part * CAP : (part + 1) * CAP, :] = packed[
                    d * CAP : (d + 1) * CAP, part * LANES : (part + 1) * LANES
                ]


def pack(owner, station, wake, owners):
    return pl.pallas_call(
        pack_kernel,
        out_shape=jax.ShapeDtypeStruct((owners, ROWS, LANES), BF16),
        compiler_params=pltpu.CompilerParams(vmem_limit_bytes=32 * 1024 * 1024),
        name="wake_pack",
    )(owner, station, wake)


def sum_kernel(got_ref, out_ref):
    sources = got_ref.shape[0]
    width = out_ref.shape[1]
    group = LANES // CAP
    total = jnp.zeros((width, 6 * LANES), F32)
    for first in range(0, sources, 2 * group):
        hots, values = [], []
        for half in range(2):
            base = first + half * group
            codes = jnp.zeros((ROWS - META, LANES), F32)
            for q in range(group):
                row = got_ref[base + q, META:ROWS, :].astype(F32)
                codes = codes + (pltpu.roll(row, q * CAP, axis=1) if q else row)
            wanted = lax.broadcasted_iota(jnp.int32, (width, LANES), 0).astype(F32) + 1.0
            hots.append(jnp.where(codes[0:1] == wanted, 1.0, 0.0).astype(BF16))
            values.append(
                jnp.concatenate(
                    [
                        got_ref[base : base + group, part * CAP : (part + 1) * CAP, :].reshape(
                            LANES, LANES
                        )
                        for part in range(6)
                    ],
                    axis=1,
                )
            )
        total = total + jnp.dot(
            jnp.concatenate(hots, axis=1),
            jnp.concatenate(values, axis=0),
            preferred_element_type=F32,
        )
    out_ref[0] = total[:, :R]
    out_ref[1] = total[:, R:]


def sum_stations(got, width):
    return pl.pallas_call(
        sum_kernel,
        out_shape=jax.ShapeDtypeStruct((2, width, R), F32),
        compiler_params=pltpu.CompilerParams(vmem_limit_bytes=32 * 1024 * 1024),
        name="wake_sum",
    )(got)


def surface_kernel(
    first_row,
    codes_ref,
    place_ref,
    own0_ref,
    own1_ref,
    own2_ref,
    chord_ref,
    inner_ref,
    outer_ref,
    inner_corner_ref,
    outer_corner_ref,
    aic_ref,
    down_ref,
    before_ref,
    after_ref,
    along_ref,
    metric_ref,
    *rest,
):
    out_ref, blocks, weights, spread, gradient, rim = rest[-6:]
    step = pl.program_id(0)
    steps = pl.num_programs(0)
    t = first_row + step
    cols = own0_ref.shape[2]
    bcols = cols // BS
    last = metric_ref.shape[1] - 1
    even = place_ref[0] == 0
    upper = first_row == 0

    @pl.when(step == 0)
    def _():
        def put(r, q, source, row, col):
            for part in range(2):
                for a in range(BC):
                    blocks[r, q, part, a * BS : (a + 1) * BS, :] = source[
                        row + a, part, col : col + BS, :
                    ]

        shift_row = 1 if upper else 0
        edge = 0 if upper else 3
        for q in range(bcols):
            put(edge, q + 1, chord_ref, 0, q * BS)
            for r, source in enumerate((own0_ref, own1_ref, own2_ref)):
                put(r + shift_row, q + 1, source, 0, q * BS)

        def sides(left, right, left_corner, right_corner):
            base = 0 if upper else BC
            put(edge, 0, left_corner, base, 0)
            put(edge, bcols + 1, right_corner, base, 0)
            for r in range(3):
                put(r + shift_row, 0, left, base + r * BC, 0)
                put(r + shift_row, bcols + 1, right, base + r * BC, 0)
            line = left.shape[0] - 2 + (0 if upper else 1)
            rim[0] = left[line].astype(F32)
            rim[1] = right[line].astype(F32)

        @pl.when(even)
        def _():
            sides(outer_ref, inner_ref, outer_corner_ref, inner_corner_ref)

        @pl.when(jnp.logical_not(even))
        def _():
            sides(inner_ref, outer_ref, inner_corner_ref, outer_corner_ref)

    diagonal = lax.broadcasted_iota(jnp.int32, (cols, cols), 0) == lax.broadcasted_iota(
        jnp.int32, (cols, cols), 1
    )

    def factor(component, i):
        line = metric_ref[component, pl.ds(i, 1), :]
        return jnp.sum(jnp.where(diagonal, line, 0.0), axis=1, keepdims=True)

    def weigh(value, column):
        return (value.astype(F32) * column).astype(BF16)

    def weigh_row(a, carry):
        column = factor(0, t * BC + a)
        for part in range(2):
            weights[a + 1, part] = weigh(down_ref[0, a, part], column)
        return carry

    lax.fori_loop(0, BC, weigh_row, 0, unroll=2)
    if upper:

        @pl.when(step == 0)
        def _():
            weights[0] = chord_ref[BC]

        @pl.when(step > 0)
        def _():
            column = factor(0, t * BC - 1)
            for part in range(2):
                weights[0, part] = weigh(before_ref[0, 0, part], column)

        column = factor(0, t * BC + BC)
        for part in range(2):
            weights[BC + 1, part] = weigh(after_ref[0, 0, part], column)
    else:

        @pl.when(step == steps - 1)
        def _():
            weights[BC + 1] = chord_ref[BC]

        @pl.when(step < steps - 1)
        def _():
            column = factor(0, t * BC + BC)
            for part in range(2):
                weights[BC + 1, part] = weigh(after_ref[0, 0, part], column)

        column = factor(0, t * BC - 1)
        for part in range(2):
            weights[0, part] = weigh(before_ref[0, 0, part], column)

    def slope_row(a, carry):
        column = factor(1, t * BC + a)
        for part in range(2):
            spread[part, 8 : 8 + cols, :] = weigh(along_ref[0, a, part], column).astype(F32)
            spread[part, 7:8, :] = rim[0, part, pl.ds(step * BC + a, 1), :]
            spread[part, 8 + cols : 9 + cols, :] = rim[1, part, pl.ds(step * BC + a, 1), :]
        for part in range(2):
            along = spread[part, 7 : 7 + cols, :] - spread[part, 9 : 9 + cols, :]
            down = weights[a, part].astype(F32) - weights[a + 2, part].astype(F32)
            gradient[a, part] = 0.5 * (down + along)
        return carry

    lax.fori_loop(0, BC, slope_row, 0, unroll=2)

    def target(u, carry):
        col = pl.multiple_of(u * BS, BS)
        for c in range(R // LANES):
            lanes = slice(c * LANES, (c + 1) * LANES)
            total = jnp.zeros((BC * BS, 2 * LANES), F32)
            for k in range(aic_ref.shape[2]):
                code = codes_ref[t, u, k]
                r = step + code // 3
                q = u + code % 3
                real = blocks[r, q, 0, :, lanes]
                imag = blocks[r, q, 1, :, lanes]
                source = jnp.concatenate(
                    [
                        jnp.concatenate([real, imag], axis=1),
                        jnp.concatenate([-imag, real], axis=1),
                    ],
                    axis=0,
                )
                matrix = jnp.concatenate([aic_ref[0, u, k, 0], aic_ref[0, u, k, 1]], axis=1)
                total = total + jnp.dot(matrix, source, preferred_element_type=F32)
            for a in range(BC):
                for part in range(2):
                    near = total[a * BS : (a + 1) * BS, part * LANES : (part + 1) * LANES]
                    slope = gradient[a, part, pl.ds(col, BS), lanes]
                    out_ref[a, part, pl.ds(col, BS), lanes] = (near + slope).astype(BF16)
        return carry

    lax.fori_loop(0, bcols, target, 0)


def surface(
    half, codes, place, own, chord, inner, outer, inner_corner, outer_corner, aic, velocity,
    metric, done=None,
):
    rows, _, cols, _ = own.shape
    brows, bcols = rows // BC, cols // BS
    steps = brows // 2
    first = half * steps
    whole = pl.BlockSpec(memory_space=pltpu.VMEM)
    scalars = pl.BlockSpec(memory_space=pltpu.SMEM)
    line = (1, 1, 2, cols, R)

    def strip(j):
        return pl.BlockSpec((BC, 2, cols, R), lambda s: (half + j, 0, 0, 0))

    arguments = [
        codes, place, own, own, own, chord, inner, outer, inner_corner, outer_corner, aic,
        velocity, velocity, velocity, velocity, metric,
    ]
    specs = (
        [scalars] * 2
        + [strip(j) for j in range(3)]
        + [whole] * 5
        + [
            pl.BlockSpec((1,) + aic.shape[1:], lambda s: (first + s, 0, 0, 0, 0, 0)),
            pl.BlockSpec((1, BC, 2, cols, R), lambda s: (0, first + s, 0, 0, 0)),
            pl.BlockSpec(line, lambda s: (0, jnp.maximum((first + s) * BC - 1, 0), 0, 0, 0)),
            pl.BlockSpec(
                line, lambda s: (0, jnp.minimum((first + s) * BC + BC, rows - 1), 0, 0, 0)
            ),
            pl.BlockSpec((1, BC, 2, cols, R), lambda s: (1, first + s, 0, 0, 0)),
            whole,
        ]
    )
    aliases = {}
    if done is not None:
        aliases = {len(arguments): 0}
        arguments.append(done)
        specs.append(pl.BlockSpec(memory_space=pl.ANY))

    def kernel(*refs):
        surface_kernel(first, *refs)

    return pl.pallas_call(
        kernel,
        grid=(steps,),
        in_specs=specs,
        out_specs=pl.BlockSpec((BC, 2, cols, R), lambda s: (first + s, 0, 0, 0)),
        out_shape=jax.ShapeDtypeStruct(own.shape, BF16),
        scratch_shapes=[
            pltpu.VMEM((4, bcols + 2, 2, BC * BS, R), BF16),
            pltpu.VMEM((BC + 2, 2, cols, R), BF16),
            pltpu.VMEM((2, cols + 16, R), F32),
            pltpu.VMEM((BC, 2, cols, R), F32),
            pltpu.VMEM((2, 2, 2 * BC, R), F32),
        ],
        input_output_aliases=aliases,
        compiler_params=pltpu.CompilerParams(vmem_limit_bytes=40 * 1024 * 1024),
        cost_estimate=pl.CostEstimate(
            flops=3_250_000_000, bytes_accessed=14_000_000, transcendentals=0
        ),
        name="surface_upper" if half == 0 else "surface_lower",
    )(*arguments)


def per_device(
    surface_adjoint,
    velocity_adjoint,
    metric,
    aic_blocks,
    block_codes,
    wake_adjoint,
    wake_owner,
    shed_station,
):
    rows, cols = surface_adjoint.shape[:2]
    owners = lax.axis_size("span")
    core = lax.axis_index("span") % 2
    own = split_parts(surface_adjoint)

    def weigh(factor, value):
        return (factor[..., None, None] * value.astype(F32)).astype(BF16)

    up_row = split_parts(weigh(metric[0, rows - 1], velocity_adjoint[0, rows - 1]))
    down_row = split_parts(weigh(metric[0, 0], velocity_adjoint[0, 0]))
    up_send = jnp.concatenate([own[rows - BC :], up_row[None]], axis=0)
    down_send = jnp.concatenate([own[:BC], down_row[None]], axis=0)
    up_send, down_send, wake, velocity_adjoint = lax.optimization_barrier(
        (up_send, down_send, wake_adjoint, velocity_adjoint)
    )
    low = shift(up_send, "chord", 1)
    high = shift(down_send, "chord", -1)

    packed = pack(
        wake_owner.reshape(1, -1), shed_station.reshape(1, -1), jnp.swapaxes(wake, 0, 1), owners
    )
    got = lax.all_to_all(packed, "span", 0, 0, tiled=True)

    inner_pairs = [(i, i ^ 1) for i in range(owners)]
    outer_pairs = [(i, i + 1) for i in range(1, owners - 1, 2)]
    outer_pairs = outer_pairs + [(j, i) for i, j in outer_pairs]
    inner_col = (1 - core) * (cols - BS)
    outer_col = core * (cols - BS)

    def side(first_col, lone_col):
        strip = lax.dynamic_slice_in_dim(own, first_col, BS, axis=2)
        lone = lax.dynamic_index_in_dim(velocity_adjoint[1], lone_col, axis=1, keepdims=False)
        scale = lax.dynamic_index_in_dim(metric[1], lone_col, axis=1, keepdims=False)
        lone = split_parts(weigh(scale, lone).reshape(rows // BS, BS, 2, R))
        return jnp.concatenate([strip, lone], axis=0)

    inner = lax.ppermute(side(inner_col, (1 - core) * (cols - 1)), "span", inner_pairs)
    outer = lax.ppermute(side(outer_col, core * (cols - 1)), "span", outer_pairs)

    def corner(first_col):
        return jnp.concatenate(
            [lax.dynamic_slice_in_dim(ref[:BC], first_col, BS, axis=2) for ref in (low, high)],
            axis=0,
        )

    inner_corner = lax.ppermute(corner(inner_col), "span", inner_pairs)
    outer_corner = lax.ppermute(corner(outer_col), "span", outer_pairs)
    velocity = split_parts(velocity_adjoint)
    place = jnp.full((1,), core, jnp.int32)
    halos = (inner, outer, inner_corner, outer_corner, aic_blocks, velocity, metric)
    summed = surface(0, block_codes, place, own, low, *halos)
    summed = surface(1, block_codes, place, own, high, *halos, done=summed)
    out = lax.optimization_barrier(split_parts(summed))

    partial = sum_stations(got, cols)
    count = lax.axis_size("chord")
    place = lax.axis_index("chord")
    half = count // 2
    pairs = [(i, 0 if i < half else count - 1) for i in (1, count - 2)]
    partial = partial + lax.ppermute(partial.astype(BF16), "chord", pairs).astype(F32)
    swap = [(0, count - 1), (count - 1, 0)]
    shed = partial + lax.ppermute(partial.astype(BF16), "chord", swap).astype(F32)
    shed = split_parts(shed)
    first = out[0].astype(F32) - jnp.where(place == 0, 1.0, 0.0) * shed
    last = out[rows - 1].astype(F32) + jnp.where(place == count - 1, 1.0, 0.0) * shed
    return out.at[0].set(first.astype(BF16)).at[rows - 1].set(last.astype(BF16))


def solution(mesh):
    in_specs = (
        P("chord", "span", None, None),
        P(None, "chord", "span", None, None),
        P(None, "chord", "span"),
        P("chord", "span", None, None, None, None),
        P("chord", "span", None),
        P(("span", "chord"), None, None),
        P(("span", "chord"), None),
        P(("span", "chord")),
    )
    out_specs = P("chord", "span", None, None)
    return jax.shard_map(
        per_device, mesh=mesh, in_specs=in_specs, out_specs=out_specs, check_vma=False
    )
```

profile of v0, /device:TPU:56, one launch (start us, length us, event | category | flops | bytes accessed | tf_op | source)
XLA Modules:
  0.0 107.5 jit_solution(7803263391278961761)
XLA Ops:
  1.8 2.6 %copy.53 = bf16[32,64,2,384]{3,1,2,0:T(8,128)(2,1)S(1)} copy(bf16[32,64,2,384]{3,2,1,0:T(2,128)(2,1)} %param.12) | data formatting | bytes 6291456 | tf_op args[0]
  6.8 1.3 %collective-permute-start.3 = (bf16[9,2,64,384]{3,2,1,0:T(8,128)(2,1)}, bf16[9,2,64,384]{3,2,1,0:T(8,128)(2,1)}, u32[]{:S(2)}, u32[]{:S(2)}) collective-permute-start(bf16[9,2,64,384]{3,2,1,0:T(8,128)(2,1)} %pad_maximum_fusion), channel_id=1, source_target_pairs={{0,1},{1,2},{2,3},{4,5},{5,6},{6,7},{8,9},{9,10},{10,11},{12,13},{... | collective-permute-start | bytes 2654216 | tf_op jit(solution)/shard_map/ppermute | solution.py:26
  8.1 5.5 %collective-permute-start = (bf16[9,2,64,384]{3,2,1,0:T(8,128)(2,1)}, bf16[9,2,64,384]{3,2,1,0:T(8,128)(2,1)}, u32[]{:S(2)}, u32[]{:S(2)}) collective-permute-start(bf16[9,2,64,384]{3,2,1,0:T(8,128)(2,1)} %pad_maximum_fusion.1), channel_id=1, source_target_pairs={{1,0},{2,1},{3,2},{5,4},{6,5},{7,6},{9,8},{10,9},{11,10},{13,12},{... | collective-permute-start | bytes 2654216 | tf_op jit(solution)/shard_map/ppermute | solution.py:26
  13.7 1.3 %wake_pack.1 = bf16[32,208,128]{2,1,0:T(8,128)(2,1)S(1)} custom-call(s32[1,512]{1,0:T(1,128)S(1)} %bitcast.85, s32[1,512]{1,0:T(1,128)S(1)} %bitcast.86, bf16[2,512,384]{2,1,0:T(8,128)(2,1)S(1)} %bitcast.84), custom_call_target="tpu_custom_call" | custom-call | tf_op jit(solution)/shard_map/wake_pack/pallas_call | solution.py:69
  15.0 1.3 %copy-done.2 = bf16[32,208,128]{2,1,0:T(8,128)(2,1)} copy-done((bf16[32,208,128]{2,1,0:T(8,128)(2,1)}, bf16[32,208,128]{2,1,0:T(8,128)(2,1)S(1)}, u32[]{:S(2)}) %copy-start.2) | copy-done | bytes 1703960
  16.3 8.1 %all-to-all-start = ((bf16[32,208,128]{2,1,0:T(8,128)(2,1)}), bf16[32,208,128]{2,1,0:T(8,128)(2,1)}, u32[]{:S(2)}, u32[]{:S(2)}) async-start(bf16[32,208,128]{2,1,0:T(8,128)(2,1)} %copy-done.2), calls=%async_computation | async-start | bytes 3407872 | tf_op jit(solution)/shard_map/all_to_all | solution.py:375
  24.4 9.8 %copy.22 = bf16[2,32,64,2,384]{4,1,3,2,0:T(8,128)(2,1)S(1)} copy(bf16[2,32,64,2,384]{4,3,2,1,0:T(2,128)(2,1)} %param.13) | data formatting | bytes 12582912 | tf_op jit(solution)/shard_map/optimization_barrier | solution.py:366
  34.1 2.0 %slice.104 = bf16[1,32,64,2,384]{4,1,3,2,0:T(8,128)(2,1)} slice(bf16[2,32,64,2,384]{4,1,3,2,0:T(8,128)(2,1)S(1)} %copy.22), slice={[1:2], [0:32], [0:64], [0:2], [0:384]} | slice | bytes 6291456 | tf_op jit(solution)/shard_map/slice | solution.py:385
  37.3 1.2 %dynamic-slice_bitcast_fusion = (bf16[32,2,16,384]{3,2,1,0:T(8,128)(2,1)S(1)}, bf16[32,2,16,384]{3,2,1,0:T(8,128)(2,1)}) fusion(bf16[32,64,2,384]{3,1,2,0:T(8,128)(2,1)S(1)} %copy.53, s32[]{:T(128)S(6)} %select_n.37, s32[]{:T(128)S(6)} %select_n.35), kind=kLoop, calls=%fused_computation.6 | loop fusion | bytes 3145736 | tf_op jit(solution)/shard_map/dynamic_slice | solution.py:384
  39.5 4.3 %collective-permute-start.2 = (bf16[34,2,16,384]{3,2,1,0:T(8,128)(2,1)}, bf16[34,2,16,384]{3,2,1,0:T(8,128)(2,1)}, u32[]{:S(2)}, u32[]{:S(2)}) collective-permute-start(bf16[34,2,16,384]{3,2,1,0:T(8,128)(2,1)} %pad_maximum_fusion.3), channel_id=1, source_target_pairs={{4,8},{12,16},{20,24},{28,32},{36,40},{44,48},{52,56},{60,64},{68,... | collective-permute-start | bytes 2506760 | tf_op jit(solution)/shard_map/ppermute | solution.py:391
  44.0 2.1 %pad_maximum_fusion.2 = bf16[34,2,16,384]{3,2,1,0:T(8,128)(2,1)} fusion(bf16[2,2,16,384]{3,2,1,0:T(8,128)(2,1)S(1)} %fusion.13, bf16[32,2,16,384]{3,2,1,0:T(8,128)(2,1)} %get-tuple-element.42), kind=kLoop, calls=%fused_computation.3 | loop fusion | flops 417792 | bytes 1671168 | tf_op jit(solution)/shard_map/concatenate | solution.py:388
  46.2 1.2 %slice.105 = bf16[8,2,64,384]{3,2,1,0:T(8,128)(2,1)S(1)} slice(bf16[9,2,64,384]{3,2,1,0:T(8,128)(2,1)} %collective-permute-done.3.refs_5_), slice={[0:8], [0:2], [0:64], [0:384]} | slice | bytes 1572864 | tf_op jit(solution)/shard_map/slice | solution.py:395
  47.4 1.2 %slice.106 = bf16[8,2,64,384]{3,2,1,0:T(8,128)(2,1)S(1)} slice(bf16[9,2,64,384]{3,2,1,0:T(8,128)(2,1)} %collective-permute-done.refs_5_), slice={[0:8], [0:2], [0:64], [0:384]} | slice | bytes 1572864 | tf_op jit(solution)/shard_map/slice | solution.py:395
  50.9 3.5 %collective-permute-start.5 = (bf16[16,2,16,384]{3,2,1,0:T(8,128)(2,1)}, bf16[16,2,16,384]{3,2,1,0:T(8,128)(2,1)}, u32[]{:S(2)}, u32[]{:S(2)}) collective-permute-start(bf16[16,2,16,384]{3,2,1,0:T(8,128)(2,1)} %pad_maximum_fusion.5), channel_id=1, source_target_pairs={{4,8},{12,16},{20,24},{28,32},{36,40},{44,48},{52,56},{60,64},{68,... | collective-permute-start | bytes 1179656 | tf_op jit(solution)/shard_map/ppermute | solution.py:400
  54.3 7.1 %copy.51 = bf16[2,32,64,2,384]{4,2,3,1,0:T(8,128)(2,1)} copy(bf16[2,32,64,2,384]{4,3,2,1,0:T(2,128)(2,1)} %param.13) | data formatting | bytes 12582912 | tf_op jit(solution)/shard_map/optimization_barrier | solution.py:366
  63.3 11.9 %surface_upper.1.refs_16_ = bf16[32,2,64,384]{3,2,1,0:T(8,128)(2,1)S(1)} custom-call(s32[4,4,8]{2,1,0:T(4,128)S(1)} %copy-done.5, s32[1]{0:T(128)} %bitcast.refs_1_, bf16[32,2,64,384]{3,2,1,0:T(8,128)(2,1)S(1)} %bitcast.75, bf16[32,2,64,384]{3,2,1,0:T(8,128)(2,1)S(1)} %bitcast.76, bf16[32,2,64,384]{3,2,1,0:T(8,128)(2,1)S(1)} %bitcast.77, ...), custom_call_target="tpu_custom_call" | custom-call | flops 3249999872 | bytes 14000000 | tf_op jit(solution)/shard_map/surface_upper/pallas_call | solution.py:322
  75.2 1.7 %copy-done = bf16[32,2,64,384]{3,2,1,0:T(8,128)(2,1)} copy-done((bf16[32,2,64,384]{3,2,1,0:T(8,128)(2,1)}, bf16[32,2,64,384]{3,2,1,0:T(8,128)(2,1)S(1)}, u32[]{:S(2)}) %copy-start) | copy-done | bytes 3145752
  76.9 1.9 %wake_sum.1 = f32[2,64,384]{2,1,0:T(8,128)S(1)} custom-call(bf16[32,208,128]{2,1,0:T(8,128)(2,1)} %all-to-all-done.got_ref), custom_call_target="tpu_custom_call" | custom-call | tf_op jit(solution)/shard_map/wake_sum/pallas_call | solution.py:113
  78.8 1.3 %collective-permute-start.6 = (bf16[2,64,384]{2,1,0:T(8,128)(2,1)S(1)}, bf16[2,64,384]{2,1,0:T(8,128)(2,1)S(1)}, u32[]{:S(2)}, u32[]{:S(2)}) collective-permute-start(bf16[2,64,384]{2,1,0:T(8,128)(2,1)S(1)} %convert_element_type.84), channel_id=1, source_target_pairs={{1,0},{2,3},{5,4},{6,7},{9,8},{10,11},{13,12},{14,15},{17,16},{18,... | collective-permute-start | bytes 294920 | tf_op jit(solution)/shard_map/ppermute | solution.py:413
  80.1 1.9 %copy-done.1 = bf16[32,2,64,384]{3,2,1,0:T(8,128)(2,1)S(1)} copy-done((bf16[32,2,64,384]{3,2,1,0:T(8,128)(2,1)S(1)}, bf16[32,2,64,384]{3,2,1,0:T(8,128)(2,1)}, u32[]{:S(2)}) %copy-start.1) | copy-done | bytes 3145752
  82.7 11.9 %surface_lower.1 = bf16[32,2,64,384]{3,2,1,0:T(8,128)(2,1)S(1)} custom-call(s32[4,4,8]{2,1,0:T(4,128)S(1)} %copy-done.5, s32[1]{0:T(128)} %bitcast.refs_1_, bf16[32,2,64,384]{3,2,1,0:T(8,128)(2,1)S(1)} %bitcast.78, bf16[32,2,64,384]{3,2,1,0:T(8,128)(2,1)S(1)} %bitcast.79, bf16[32,2,64,384]{3,2,1,0:T(8,128)(2,1)S(1)} %bitcast.80, ...), custom_call_target="tpu_custom_call", output_to_operand_aliasing={{}: (16, {})} | custom-call | flops 3249999872 | bytes 14000000 | tf_op jit(solution)/shard_map/surface_lower/pallas_call | solution.py:322
  94.7 1.9 %collective-permute-start.7 = (bf16[2,64,384]{2,1,0:T(8,128)(2,1)S(1)}, bf16[2,64,384]{2,1,0:T(8,128)(2,1)S(1)}, u32[]{:S(2)}, u32[]{:S(2)}) collective-permute-start(bf16[2,64,384]{2,1,0:T(8,128)(2,1)S(1)} %fusion.4), channel_id=1, source_target_pairs={{0,3},{3,0},{4,7},{7,4},{8,11},{11,8},{12,15},{15,12},{16,19},{19,... | collective-permute-start | bytes 294920 | tf_op jit(solution)/shard_map/ppermute | solution.py:415
  97.2 5.2 %collective-permute-done.7 = bf16[2,64,384]{2,1,0:T(8,128)(2,1)S(1)} collective-permute-done((bf16[2,64,384]{2,1,0:T(8,128)(2,1)S(1)}, bf16[2,64,384]{2,1,0:T(8,128)(2,1)S(1)}, u32[]{:S(2)}, u32[]{:S(2)}) %collective-permute-start.7) | collective-permute-done | bytes 98336 | tf_op jit(solution)/shard_map/ppermute | solution.py:415
  102.6 4.9 %copy.28 = bf16[32,64,2,384]{3,2,1,0:T(2,128)(2,1)} copy(bf16[32,64,2,384]{3,1,2,0:T(8,128)(2,1)S(1)} %fusion.10) | data formatting | bytes 6291456 | tf_op jit(solution)/shard_map/scatter | solution.py:419
  (51 shorter events, 12.2 us)
Async XLA Ops:
  4.4 9.2 %copy-start.8 = (bf16[512,2,384]{2,1,0:T(2,128)(2,1)S(1)}, bf16[512,2,384]{2,1,0:T(2,128)(2,1)}, u32[]{:S(2)}) copy-start(bf16[512,2,384]{2,1,0:T(2,128)(2,1)} %param.17) | copy-start | bytes 2359300
  4.6 9.1 %copy-start.6 = (s32[512,1]{0,1:T(1,128)S(1)}, s32[512,1]{0,1:T(1,128)}, u32[]{:S(2)}) copy-start(s32[512,1]{0,1:T(1,128)} %param.18) | copy-start | bytes 6148
  4.6 9.1 %copy-start.7 = (s32[512]{0:T(512)S(1)}, s32[512]{0:T(512)}, u32[]{:S(2)}) copy-start(s32[512]{0:T(512)} %param.19) | copy-start | bytes 6148
  6.8 39.3 %collective-permute-start.3 = (bf16[9,2,64,384]{3,2,1,0:T(8,128)(2,1)}, bf16[9,2,64,384]{3,2,1,0:T(8,128)(2,1)}, u32[]{:S(2)}, u32[]{:S(2)}) collective-permute-start(bf16[9,2,64,384]{3,2,1,0:T(8,128)(2,1)} %pad_maximum_fusion), channel_id=1, source_target_pairs={{0,1},{1,2},{2,3},{4,5},{5,6},{6,7},{8,9},{9,10},{10,11},{12,13},{... | collective-permute-start | bytes 2654216 | tf_op jit(solution)/shard_map/ppermute | solution.py:26
  8.1 39.3 %collective-permute-start = (bf16[9,2,64,384]{3,2,1,0:T(8,128)(2,1)}, bf16[9,2,64,384]{3,2,1,0:T(8,128)(2,1)}, u32[]{:S(2)}, u32[]{:S(2)}) collective-permute-start(bf16[9,2,64,384]{3,2,1,0:T(8,128)(2,1)} %pad_maximum_fusion.1), channel_id=1, source_target_pairs={{1,0},{2,1},{3,2},{5,4},{6,5},{7,6},{9,8},{10,9},{11,10},{13,12},{... | collective-permute-start | bytes 2654216 | tf_op jit(solution)/shard_map/ppermute | solution.py:26
  15.0 1.3 %copy-start.2 = (bf16[32,208,128]{2,1,0:T(8,128)(2,1)}, bf16[32,208,128]{2,1,0:T(8,128)(2,1)S(1)}, u32[]{:S(2)}) copy-start(bf16[32,208,128]{2,1,0:T(8,128)(2,1)S(1)} %wake_pack.1) | copy-start | bytes 5111812
  16.3 60.6 %all-to-all-start = ((bf16[32,208,128]{2,1,0:T(8,128)(2,1)}), bf16[32,208,128]{2,1,0:T(8,128)(2,1)}, u32[]{:S(2)}, u32[]{:S(2)}) async-start(bf16[32,208,128]{2,1,0:T(8,128)(2,1)} %copy-done.2), calls=%async_computation | async-start | bytes 3407872 | tf_op jit(solution)/shard_map/all_to_all | solution.py:375
  34.1 2.9 %slice-start = ((f32[2,32,64]{2,1,0:T(8,128)}), f32[1,32,64]{2,1,0:T(8,128)S(1)}, s32[]{:S(2)}) async-start(f32[2,32,64]{2,1,0:T(8,128)} %refs_15_.3), calls=%async_computation.1 | async-start | bytes 32768 | tf_op jit(solution)/shard_map/slice | solution.py:386
  39.5 21.9 %collective-permute-start.2 = (bf16[34,2,16,384]{3,2,1,0:T(8,128)(2,1)}, bf16[34,2,16,384]{3,2,1,0:T(8,128)(2,1)}, u32[]{:S(2)}, u32[]{:S(2)}) collective-permute-start(bf16[34,2,16,384]{3,2,1,0:T(8,128)(2,1)} %pad_maximum_fusion.3), channel_id=1, source_target_pairs={{4,8},{12,16},{20,24},{28,32},{36,40},{44,48},{52,56},{60,64},{68,... | collective-permute-start | bytes 2506760 | tf_op jit(solution)/shard_map/ppermute | solution.py:391
  46.2 15.3 %collective-permute-start.1 = (bf16[34,2,16,384]{3,2,1,0:T(8,128)(2,1)}, bf16[34,2,16,384]{3,2,1,0:T(8,128)(2,1)}, u32[]{:S(2)}, u32[]{:S(2)}) collective-permute-start(bf16[34,2,16,384]{3,2,1,0:T(8,128)(2,1)} %pad_maximum_fusion.2), channel_id=1, source_target_pairs={{0,4},{4,0},{8,12},{12,8},{16,20},{20,16},{24,28},{28,24},{32,36},... | collective-permute-start | bytes 2506760 | tf_op jit(solution)/shard_map/ppermute | solution.py:390
  49.6 11.9 %collective-permute-start.4 = (bf16[16,2,16,384]{3,2,1,0:T(8,128)(2,1)}, bf16[16,2,16,384]{3,2,1,0:T(8,128)(2,1)S(1)}, u32[]{:S(2)}, u32[]{:S(2)}) collective-permute-start(bf16[16,2,16,384]{3,2,1,0:T(8,128)(2,1)} %pad_maximum_fusion.4), channel_id=1, source_target_pairs={{0,4},{4,0},{8,12},{12,8},{16,20},{20,16},{24,28},{28,24},{32,36},... | collective-permute-start | bytes 1179656 | tf_op jit(solution)/shard_map/ppermute | solution.py:399
  50.9 11.6 %copy-start.5 = (s32[4,4,8]{2,1,0:T(4,128)S(1)}, s32[4,4,8]{2,1,0:T(4,128)}, u32[]{:S(2)}) copy-start(s32[4,4,8]{2,1,0:T(4,128)} %refs_0_.3) | copy-start | bytes 1540
  50.9 11.6 %collective-permute-start.5 = (bf16[16,2,16,384]{3,2,1,0:T(8,128)(2,1)}, bf16[16,2,16,384]{3,2,1,0:T(8,128)(2,1)}, u32[]{:S(2)}, u32[]{:S(2)}) collective-permute-start(bf16[16,2,16,384]{3,2,1,0:T(8,128)(2,1)} %pad_maximum_fusion.5), channel_id=1, source_target_pairs={{4,8},{12,16},{20,24},{28,32},{36,40},{44,48},{52,56},{60,64},{68,... | collective-permute-start | bytes 1179656 | tf_op jit(solution)/shard_map/ppermute | solution.py:400
  62.5 0.8 copy-start.3
  75.2 1.7 %copy-start = (bf16[32,2,64,384]{3,2,1,0:T(8,128)(2,1)}, bf16[32,2,64,384]{3,2,1,0:T(8,128)(2,1)S(1)}, u32[]{:S(2)}) copy-start(bf16[32,2,64,384]{3,2,1,0:T(8,128)(2,1)S(1)} %surface_upper.1.refs_16_) | copy-start | bytes 9437188
  78.8 15.9 %collective-permute-start.6 = (bf16[2,64,384]{2,1,0:T(8,128)(2,1)S(1)}, bf16[2,64,384]{2,1,0:T(8,128)(2,1)S(1)}, u32[]{:S(2)}, u32[]{:S(2)}) collective-permute-start(bf16[2,64,384]{2,1,0:T(8,128)(2,1)S(1)} %convert_element_type.84), channel_id=1, source_target_pairs={{1,0},{2,3},{5,4},{6,7},{9,8},{10,11},{13,12},{14,15},{17,16},{18,... | collective-permute-start | bytes 294920 | tf_op jit(solution)/shard_map/ppermute | solution.py:413
  80.1 1.9 %copy-start.1 = (bf16[32,2,64,384]{3,2,1,0:T(8,128)(2,1)S(1)}, bf16[32,2,64,384]{3,2,1,0:T(8,128)(2,1)}, u32[]{:S(2)}) copy-start(bf16[32,2,64,384]{3,2,1,0:T(8,128)(2,1)} %copy-done) | copy-start | bytes 9437188
  82.0 0.8 copy-start.4
  94.7 7.7 %collective-permute-start.7 = (bf16[2,64,384]{2,1,0:T(8,128)(2,1)S(1)}, bf16[2,64,384]{2,1,0:T(8,128)(2,1)S(1)}, u32[]{:S(2)}, u32[]{:S(2)}) collective-permute-start(bf16[2,64,384]{2,1,0:T(8,128)(2,1)S(1)} %fusion.4), channel_id=1, source_target_pairs={{0,3},{3,0},{4,7},{7,4},{8,11},{11,8},{12,15},{15,12},{16,19},{19,... | collective-permute-start | bytes 294920 | tf_op jit(solution)/shard_map/ppermute | solution.py:415
where the time goes:
time: 108 us; the launch traced here: 107 us
  local copies, waits for them, and re-layouts  40.2 us (37%)
  Pallas kernels  27 us (25%)
  starting transfers between devices  26.4 us (24%)
  other arithmetic  7.28 us (7%)
  waiting for transfers between devices  6.34 us (6%)
    pallas_call x2, Pallas kernels, surface(): pl.pallas_call(kernel, grid=(steps,), in_specs=specs, out_specs=pl.BlockS...  23.8 us
    optimization_barrier x3, local copies, waits for them, and re-layouts, per_device(): lax.optimization_barrier((up_send, down_send, wake_adjoint, velocity_adjo...  16.9 us
    unnamed x21, local copies, waits for them, and re-layouts  9.48 us
    all_to_all x1, starting transfers between devices, per_device(): got = lax.all_to_all(packed, 'span', 0, 0, tiled=True)  8.09 us
    ppermute x2, starting transfers between devices, shift(): return lax.ppermute(array, axis, pairs)  6.77 us
    ppermute x1, waiting for transfers between devices, per_device(): lax.ppermute(partial.astype(BF16), 'chord', swap).astype(F32)  5.24 us
    scatter x1, local copies, waits for them, and re-layouts, per_device(): return out.at[0].set(first.astype(BF16)).at[rows - 1].set(last.astype(BF16))  4.9 us
    ppermute x1, starting transfers between devices, per_device(): lax.ppermute(side(outer_col, core * (cols - 1)), 'span', outer_pairs)  4.32 us
  transfers between devices with their start and end apart: 9, of which 2 were waited for; matrix products, arithmetic and copies ran while one was open for 27% of the time, Pallas kernels for 23%

commit v1 on v0

v1 whole, which is shorter than its diff:
```python
import jax
import jax.numpy as jnp
from jax import lax
from jax.experimental import pallas as pl
from jax.experimental.pallas import tpu as pltpu
from jax.sharding import PartitionSpec as P

BC = 8
BS = 16
R = 384
CAP = 32
LANES = 128
META = 192
ROWS = 208
F32 = jnp.float32
BF16 = jnp.bfloat16


def split_parts(array):
    return jnp.swapaxes(array, -3, -2)


def shift(array, axis, step):
    count = lax.axis_size(axis)
    pairs = [(i, i + step) for i in range(count) if 0 <= i + step < count]
    return lax.ppermute(array, axis, pairs)


def pack_kernel(owner_ref, station_ref, wake_ref, out_ref):
    rows = owner_ref.shape[1]
    owners = out_ref.shape[0]
    owner = owner_ref[...]
    station = station_ref[...]
    named = lax.broadcasted_iota(jnp.int32, (owners, rows), 0) == owner
    hot = jnp.where(named, 1.0, 0.0).astype(F32)
    before = jnp.where(
        lax.broadcasted_iota(jnp.int32, (rows, rows), 0)
        < lax.broadcasted_iota(jnp.int32, (rows, rows), 1),
        1.0,
        0.0,
    ).astype(BF16)
    counts = jnp.dot(hot.astype(BF16), before, preferred_element_type=F32)
    rank = jnp.sum(hot * counts, axis=0, keepdims=True).astype(jnp.int32)
    slot = owner * CAP + rank
    stations = jnp.where(named, (station + 1).astype(F32), 0.0).astype(BF16)
    ranks = jnp.where(
        lax.broadcasted_iota(jnp.int32, (LANES, rows), 0) == rank, 1.0, 0.0
    ).astype(BF16)
    meta = lax.dot_general(
        stations, ranks, (((1,), (1,)), ((), ())), preferred_element_type=F32
    ).astype(BF16)
    for d in range(owners):
        out_ref[d, META:ROWS, :] = jnp.broadcast_to(meta[d : d + 1], (ROWS - META, LANES))
    values = jnp.concatenate([wake_ref[0], wake_ref[1]], axis=1)
    chunk = 256
    for first in range(0, owners * CAP, chunk):
        place = jnp.where(
            lax.broadcasted_iota(jnp.int32, (chunk, rows), 0) + first == slot, 1.0, 0.0
        ).astype(BF16)
        packed = jnp.dot(place, values, preferred_element_type=F32).astype(BF16)
        for d in range(chunk // CAP):
            for part in range(6):
                out_ref[first // CAP + d, part * CAP : (part + 1) * CAP, :] = packed[
                    d * CAP : (d + 1) * CAP, part * LANES : (part + 1) * LANES
                ]


def pack(owner, station, wake, owners):
    return pl.pallas_call(
        pack_kernel,
        out_shape=jax.ShapeDtypeStruct((owners, ROWS, LANES), BF16),
        compiler_params=pltpu.CompilerParams(vmem_limit_bytes=32 * 1024 * 1024),
        name="wake_pack",
    )(owner, station, wake)


def sum_kernel(got_ref, out_ref):
    sources = got_ref.shape[0]
    width = out_ref.shape[1]
    group = LANES // CAP
    total = jnp.zeros((width, 6 * LANES), F32)
    for first in range(0, sources, 2 * group):
        hots, values = [], []
        for half in range(2):
            base = first + half * group
            codes = jnp.zeros((ROWS - META, LANES), F32)
            for q in range(group):
                row = got_ref[base + q, META:ROWS, :].astype(F32)
                codes = codes + (pltpu.roll(row, q * CAP, axis=1) if q else row)
            wanted = lax.broadcasted_iota(jnp.int32, (width, LANES), 0).astype(F32) + 1.0
            hots.append(jnp.where(codes[0:1] == wanted, 1.0, 0.0).astype(BF16))
            values.append(
                jnp.concatenate(
                    [
                        got_ref[base : base + group, part * CAP : (part + 1) * CAP, :].reshape(
                            LANES, LANES
                        )
                        for part in range(6)
                    ],
                    axis=1,
                )
            )
        total = total + jnp.dot(
            jnp.concatenate(hots, axis=1),
            jnp.concatenate(values, axis=0),
            preferred_element_type=F32,
        )
    out_ref[0] = total[:, :R]
    out_ref[1] = total[:, R:]


def sum_stations(got, width):
    return pl.pallas_call(
        sum_kernel,
        out_shape=jax.ShapeDtypeStruct((2, width, R), F32),
        compiler_params=pltpu.CompilerParams(vmem_limit_bytes=32 * 1024 * 1024),
        name="wake_sum",
    )(got)


def surface_kernel(
    inside,
    codes_ref,
    place_ref,
    own_ref,
    low_ref,
    high_ref,
    inner_ref,
    outer_ref,
    inner_corner_ref,
    outer_corner_ref,
    aic_ref,
    down_ref,
    before_ref,
    after_ref,
    along_ref,
    metric_ref,
    *rest,
):
    out_ref, blocks, factors, stage, weights, spread, gradient, rim, chord_row, mixed = rest[-10:]
    step = pl.program_id(0)
    c = pl.program_id(1)
    steps = pl.num_programs(0)
    t = target_row(inside, step)
    cols = own_ref.shape[2]
    brows = own_ref.shape[0] // BC
    bcols = cols // BS
    rows = metric_ref.shape[1]
    even = place_ref[0] == 0
    lane_sets = [slice(n * LANES, (n + 1) * LANES) for n in range(R // LANES)]

    @pl.when((step == 0) & (c == 0))
    def _():
        def put(r, q, source, row, col):
            for n, lanes in enumerate(lane_sets):
                for part in range(2):
                    for a in range(BC):
                        blocks[r, q, n, part, a * BS : (a + 1) * BS, :] = source[
                            row + a, part, col : col + BS, lanes
                        ]

        for q in range(bcols):
            for r in range(brows):
                put(r + 1, q + 1, own_ref, r * BC, q * BS)
            if not inside:
                put(0, q + 1, low_ref, 0, q * BS)
                put(brows + 1, q + 1, high_ref, 0, q * BS)
        if not inside:
            for n, lanes in enumerate(lane_sets):
                for part in range(2):
                    chord_row[0, n, part] = low_ref[BC, part, :, lanes]
                    chord_row[1, n, part] = high_ref[BC, part, :, lanes]

        def sides(left, right, left_corner, right_corner):
            for r in range(brows):
                put(r + 1, 0, left, r * BC, 0)
                put(r + 1, bcols + 1, right, r * BC, 0)
            if not inside:
                put(0, 0, left_corner, 0, 0)
                put(brows + 1, 0, left_corner, BC, 0)
                put(0, bcols + 1, right_corner, 0, 0)
                put(brows + 1, bcols + 1, right_corner, BC, 0)
            for piece in range(rows // BS):
                here = slice(piece * BS, (piece + 1) * BS)
                for n, lanes in enumerate(lane_sets):
                    for part in range(2):
                        rim[n, 0, part, here] = left[rows + piece, part, :, lanes].astype(F32)
                        rim[n, 1, part, here] = right[rows + piece, part, :, lanes].astype(F32)

        @pl.when(even)
        def _():
            sides(outer_ref, inner_ref, outer_corner_ref, inner_corner_ref)

        @pl.when(jnp.logical_not(even))
        def _():
            sides(inner_ref, outer_ref, inner_corner_ref, outer_corner_ref)

    @pl.when(c == 0)
    def _():
        diagonal = lax.broadcasted_iota(jnp.int32, (cols, cols), 0) == lax.broadcasted_iota(
            jnp.int32, (cols, cols), 1
        )
        for component in range(2):
            for a in range(component, BC + 2 - component):
                i = jnp.clip(t * BC - 1 + a, 0, rows - 1)
                line = metric_ref[component, pl.ds(i, 1), :]
                column = jnp.sum(jnp.where(diagonal, line, 0.0), axis=1, keepdims=True)
                factors[component, a] = jnp.broadcast_to(column, (cols, LANES))

    def weighted(ref, slot, factor):
        stage[slot] = ref.reshape(2 * cols, LANES)[...].astype(F32)
        return [stage[slot, pl.ds(part, cols, stride=2), :] * factor for part in range(2)]

    sources = [before_ref.at[0, 0]] + [down_ref.at[0, a] for a in range(BC)] + [after_ref.at[0, 0]]
    for a, source in enumerate(sources):
        pair = weighted(source, a, factors[0, a])
        for part in range(2):
            weights[a, part] = pair[part].astype(BF16)

    if not inside:

        @pl.when(step == 0)
        def _():
            weights[0] = chord_row[0, c]

        @pl.when(step == steps - 1)
        def _():
            weights[BC + 1] = chord_row[1, c]

    for a in range(BC):
        pair = weighted(along_ref.at[0, a], BC + 2 + a, factors[1, a + 1])
        for part in range(2):
            line = spread.at[a, part]
            line[8 : 8 + cols, :] = pair[part]
            line[7:8, :] = rim[c, 0, part, pl.ds(t * BC + a, 1), :]
            line[8 + cols : 9 + cols, :] = rim[c, 1, part, pl.ds(t * BC + a, 1), :]
            along = line[7 : 7 + cols, :] - line[9 : 9 + cols, :]
            down = weights[a, part].astype(F32) - weights[a + 2, part].astype(F32)
            gradient[a, part] = 0.5 * (down + along)

    for u in range(bcols):
        total = jnp.zeros((BC * BS, 2 * LANES), F32)
        for k in range(aic_ref.shape[2]):
            code = codes_ref[t, u, k]
            r = t + code // 3
            q = u + code % 3
            real = blocks[r, q, c, 0]
            imag = blocks[r, q, c, 1]
            source = jnp.concatenate(
                [
                    jnp.concatenate([real, imag], axis=1),
                    jnp.concatenate([-imag, real], axis=1),
                ],
                axis=0,
            )
            matrix = jnp.concatenate([aic_ref[0, u, k, 0], aic_ref[0, u, k, 1]], axis=1)
            total = total + jnp.dot(matrix, source, preferred_element_type=F32)
        for a in range(BC):
            for part in range(2):
                near = total[a * BS : (a + 1) * BS, part * LANES : (part + 1) * LANES]
                slope = gradient[a, part, u * BS : (u + 1) * BS, :]
                mixed[a, pl.ds(2 * u * BS + part, BS, stride=2), :] = near + slope
    for a in range(BC):
        out_ref.at[a].reshape(2 * cols, LANES)[...] = mixed[a].astype(BF16)


def target_row(inside, step):
    return step + 1 if inside else 3 * step


def surface(inside, codes, place, own, halos, aic, velocity, metric, done=None):
    rows, _, cols, _ = own.shape
    brows, bcols = rows // BC, cols // BS

    def whole(array):
        return pl.BlockSpec(array.shape, lambda s, c: (0,) * array.ndim)

    scalars = pl.BlockSpec(memory_space=pltpu.SMEM)
    line = (1, 1, cols, 2, LANES)
    strips = (1, BC, cols, 2, LANES)

    def row(s):
        return target_row(inside, s)

    def before(s, c):
        return (0, jnp.maximum(row(s) * BC - 1, 0), 0, 0, c)

    def after(s, c):
        return (0, jnp.minimum(row(s) * BC + BC, rows - 1), 0, 0, c)

    arguments = [codes, place, own, *halos, aic, velocity, velocity, velocity, velocity, metric]
    specs = (
        [scalars] * 2
        + [whole(array) for array in (own, *halos)]
        + [
            pl.BlockSpec((1,) + aic.shape[1:], lambda s, c: (row(s), 0, 0, 0, 0, 0)),
            pl.BlockSpec(strips, lambda s, c: (0, row(s), 0, 0, c)),
            pl.BlockSpec(line, before),
            pl.BlockSpec(line, after),
            pl.BlockSpec(strips, lambda s, c: (1, row(s), 0, 0, c)),
            whole(metric),
        ]
    )
    aliases = {}
    if done is not None:
        aliases = {len(arguments): 0}
        arguments.append(done)
        specs.append(pl.BlockSpec(memory_space=pl.ANY))

    def kernel(*refs):
        if inside:
            refs = refs[:3] + (None, None) + refs[3:5] + (None, None) + refs[5:]
        surface_kernel(inside, *refs)

    return pl.pallas_call(
        kernel,
        grid=(brows // 2, R // LANES),
        in_specs=specs,
        out_specs=pl.BlockSpec((BC, cols, 2, LANES), lambda s, c: (row(s), 0, 0, c)),
        out_shape=jax.ShapeDtypeStruct((rows, cols, 2, R), BF16),
        scratch_shapes=[
            pltpu.VMEM((brows + 2, bcols + 2, R // LANES, 2, BC * BS, LANES), BF16),
            pltpu.VMEM((2, BC + 2, cols, LANES), F32),
            pltpu.VMEM((2 * BC + 2, 2 * cols, LANES), F32),
            pltpu.VMEM((BC + 2, 2, cols, LANES), BF16),
            pltpu.VMEM((BC, 2, cols + 16, LANES), F32),
            pltpu.VMEM((BC, 2, cols, LANES), F32),
            pltpu.VMEM((R // LANES, 2, 2, rows, LANES), F32),
            pltpu.VMEM((2, R // LANES, 2, cols, LANES), BF16),
            pltpu.VMEM((BC, 2 * cols, LANES), F32),
        ],
        input_output_aliases=aliases,
        compiler_params=pltpu.CompilerParams(vmem_limit_bytes=56 * 1024 * 1024),
        cost_estimate=pl.CostEstimate(
            flops=3_250_000_000, bytes_accessed=14_000_000, transcendentals=0
        ),
        name="surface_inside" if inside else "surface_rim",
    )(*arguments)


def per_device(
    surface_adjoint,
    velocity_adjoint,
    metric,
    aic_blocks,
    block_codes,
    wake_adjoint,
    wake_owner,
    shed_station,
):
    rows, cols = surface_adjoint.shape[:2]
    owners = lax.axis_size("span")
    core = lax.axis_index("span") % 2
    own = split_parts(surface_adjoint)

    def weigh(factor, value):
        return (factor[..., None, None] * value.astype(F32)).astype(BF16)

    up_row = split_parts(weigh(metric[0, rows - 1], velocity_adjoint[0, rows - 1]))
    down_row = split_parts(weigh(metric[0, 0], velocity_adjoint[0, 0]))
    up_send = jnp.concatenate([own[rows - BC :], up_row[None]], axis=0)
    down_send = jnp.concatenate([own[:BC], down_row[None]], axis=0)
    inner_pairs = [(i, i ^ 1) for i in range(owners)]
    outer_pairs = [(i, i + 1) for i in range(1, owners - 1, 2)]
    outer_pairs = outer_pairs + [(j, i) for i, j in outer_pairs]
    inner_col = (1 - core) * (cols - BS)
    outer_col = core * (cols - BS)

    def side(first_col, lone_col):
        strip = lax.dynamic_slice_in_dim(own, first_col, BS, axis=2)
        lone = lax.dynamic_slice(velocity_adjoint, (1, 0, lone_col, 0, 0), (1, rows, 1, 2, R))
        lone = lone[0, :, 0]
        scale = lax.dynamic_slice(metric, (1, 0, lone_col), (1, rows, 1))[0, :, 0]
        lone = split_parts(weigh(scale, lone).reshape(rows // BS, BS, 2, R))
        return jnp.concatenate([strip, lone], axis=0)

    inner_send = side(inner_col, (1 - core) * (cols - 1))
    outer_send = side(outer_col, core * (cols - 1))
    inner = lax.ppermute(inner_send, "span", inner_pairs)
    outer = lax.ppermute(outer_send, "span", outer_pairs)
    up_send, down_send, wake = lax.optimization_barrier((up_send, down_send, wake_adjoint))
    low = shift(up_send, "chord", 1)
    high = shift(down_send, "chord", -1)

    packed = pack(
        wake_owner.reshape(1, -1), shed_station.reshape(1, -1), jnp.swapaxes(wake, 0, 1), owners
    )
    packed, inner, outer = lax.optimization_barrier((packed, inner, outer))
    got = lax.all_to_all(packed, "span", 0, 0, tiled=True)

    place = jnp.full((1,), core, jnp.int32)
    shared = (aic_blocks, velocity_adjoint, metric)
    out = surface(True, block_codes, place, own, (inner, outer), *shared)
    low, high, out = lax.optimization_barrier((low, high, out))

    def corner(first_col):
        return jnp.concatenate(
            [lax.dynamic_slice(ref, (0, 0, first_col, 0), (BC, 2, BS, R)) for ref in (low, high)],
            axis=0,
        )

    inner_corner = lax.ppermute(corner(inner_col), "span", inner_pairs)
    outer_corner = lax.ppermute(corner(outer_col), "span", outer_pairs)
    halos = (low, high, inner, outer, inner_corner, outer_corner)
    out = surface(False, block_codes, place, own, halos, *shared, done=out)

    partial = sum_stations(got, cols)
    count = lax.axis_size("chord")
    place = lax.axis_index("chord")
    half = count // 2
    pairs = [(i, 0 if i < half else count - 1) for i in (1, count - 2)]
    partial = partial + lax.ppermute(partial.astype(BF16), "chord", pairs).astype(F32)
    swap = [(0, count - 1), (count - 1, 0)]
    shed = partial + lax.ppermute(partial.astype(BF16), "chord", swap).astype(F32)
    shed = split_parts(shed)
    first = out[0].astype(F32) - jnp.where(place == 0, 1.0, 0.0) * shed
    last = out[rows - 1].astype(F32) + jnp.where(place == count - 1, 1.0, 0.0) * shed
    return out.at[0].set(first.astype(BF16)).at[rows - 1].set(last.astype(BF16))


def solution(mesh):
    in_specs = (
        P("chord", "span", None, None),
        P(None, "chord", "span", None, None),
        P(None, "chord", "span"),
        P("chord", "span", None, None, None, None),
        P("chord", "span", None),
        P(("span", "chord"), None, None),
        P(("span", "chord"), None),
        P(("span", "chord")),
    )
    out_specs = P("chord", "span", None, None)
    return jax.shard_map(
        per_device, mesh=mesh, in_specs=in_specs, out_specs=out_specs, check_vma=False
    )
```

time: 108 us -> 85 us (0.79)
  local copies, waits for them, and re-layouts: 40.2 us -> 9.2 us
  Pallas kernels: 27 us -> 34 us
  waiting for transfers between devices: 6.34 us -> 9.11 us
  starting transfers between devices: 26.4 us -> 25.3 us
    optimization_barrier x3 -> x1, local copies, waits for them, and re-layouts: 16.9 us -> 0.1 us  [per_device(): lax.optimization_barrier((up_send, down_send, wake_adjoint))]
    pallas_call x2, Pallas kernels: 23.8 us -> 31 us  [surface(): pl.pallas_call(kernel, grid=(brows // 2, R // LANES), in_specs=specs, out...]
    unnamed x21 -> x17, local copies, waits for them, and re-layouts: 9.48 us -> 2.65 us
    scatter x1 -> x2, local copies, waits for them, and re-layouts: 4.9 us -> 1.49 us  [per_device(): return out.at[0].set(first.astype(BF16)).at[rows - 1].set(last.astype(BF16))]
    slice x5 -> x1, local copies, waits for them, and re-layouts: 4.45 us -> 1.08 us  [per_device(): out[rows - 1].astype(F32) + jnp.where(place == count - 1, 1.0, 0.0) * shed]
    all_to_all x1, waiting for transfers between devices: 0.01 us -> 1.78 us  [per_device(): got = lax.all_to_all(packed, 'span', 0, 0, tiled=True)]
    ppermute x1, waiting for transfers between devices: 1.09 us -> 2.81 us  [per_device(): outer_corner = lax.ppermute(corner(outer_col), 'span', outer_pairs)]
    pallas_call x1, Pallas kernels: 1.88 us -> 0.43 us  [sum_stations(): pl.pallas_call(sum_kernel, out_shape=jax.ShapeDtypeStruct((2, width, R),...]
  transfers between devices with their start and end apart: 9 -> 9, of which waited for: 2 -> 3; matrix products, arithmetic and copies ran while one was open for 27% -> 9% of each run, Pallas kernels for 23% -> 40%
where the time goes in v1:
time: 85 us; the launch traced here: 84.4 us
  Pallas kernels  34 us (40%)
  starting transfers between devices  25.3 us (30%)
  local copies, waits for them, and re-layouts  9.2 us (11%)
  waiting for transfers between devices  9.11 us (11%)
  other arithmetic  6.51 us (8%)
    pallas_call x2, Pallas kernels, surface(): pl.pallas_call(kernel, grid=(brows // 2, R // LANES), in_specs=specs, out...  31 us
    all_to_all x1, starting transfers between devices, per_device(): got = lax.all_to_all(packed, 'span', 0, 0, tiled=True)  7.37 us
    ppermute x2, starting transfers between devices, shift(): return lax.ppermute(array, axis, pairs)  5.88 us
    ppermute x1, waiting for transfers between devices, per_device(): lax.ppermute(partial.astype(BF16), 'chord', swap).astype(F32)  4.5 us
    ppermute x1, starting transfers between devices, per_device(): outer_corner = lax.ppermute(corner(outer_col), 'span', outer_pairs)  4.34 us
    ppermute x1, starting transfers between devices, per_device(): outer = lax.ppermute(outer_send, 'span', outer_pairs)  4.32 us
    ppermute x1, waiting for transfers between devices, per_device(): outer_corner = lax.ppermute(corner(outer_col), 'span', outer_pairs)  2.81 us
    unnamed x17, local copies, waits for them, and re-layouts  2.65 us
  transfers between devices with their start and end apart: 9, of which 3 were waited for; matrix products, arithmetic and copies ran while one was open for 9% of the time, Pallas kernels for 40%

profile of v1, /device:TPU:56, one launch (start us, length us, event | category | flops | bytes accessed | tf_op | source)
XLA Modules:
  0.0 84.4 jit_solution(8770911061728273470)
XLA Ops:
  0.0 2.6 %copy.68 = bf16[32,64,2,384]{3,1,2,0:T(8,128)(2,1)S(1)} copy(bf16[32,64,2,384]{3,2,1,0:T(2,128)(2,1)} %param.12) | data formatting | bytes 6291456 | tf_op args[0]
  2.6 1.0 %constant_dynamic-slice_fusion.4 = (bf16[1,32,1,2,384]{4,3,2,1,0:T(2,128)(2,1)S(1)}, bf16[1,32,1,2,384]{4,3,2,1,0:T(2,128)(2,1)S(1)}) fusion(bf16[2,32,64,2,384]{4,3,2,1,0:T(2,128)(2,1)} %refs_13_.1, s32[]{:T(128)S(6)} %select_n.36, s32[]{:T(128)S(6)} %select_n.34), kind=kLoop, calls=%fused_computation.42 | loop fusion | bytes 196616 | tf_op jit(solution)/shard_map/dynamic_slice | solution.py:371
  4.0 1.1 %dynamic-slice_bitcast_fusion = (bf16[32,2,16,384]{3,2,1,0:T(8,128)(2,1)}, bf16[32,2,16,384]{3,2,1,0:T(8,128)(2,1)S(1)}) fusion(bf16[32,64,2,384]{3,1,2,0:T(8,128)(2,1)S(1)} %copy.68, s32[]{:T(128)S(6)} %select_n.35, s32[]{:T(128)S(6)} %select_n.33), kind=kLoop, calls=%fused_computation.5 | loop fusion | bytes 3145736 | tf_op jit(solution)/shard_map/dynamic_slice | solution.py:370
  5.2 1.0 %pad_maximum_fusion.2 = bf16[34,2,16,384]{3,2,1,0:T(8,128)(2,1)} fusion(bf16[2,2,16,384]{3,2,1,0:T(8,128)(2,1)S(1)} %fusion.11, bf16[32,2,16,384]{3,2,1,0:T(8,128)(2,1)S(1)} %get-tuple-element.56), kind=kLoop, calls=%fused_computation.2 | loop fusion | flops 417792 | bytes 1671168 | tf_op jit(solution)/shard_map/concatenate | solution.py:375
  6.3 1.2 %pad_maximum_fusion.3 = bf16[34,2,16,384]{3,2,1,0:T(8,128)(2,1)S(1)} fusion(bf16[2,2,16,384]{3,2,1,0:T(8,128)(2,1)S(1)} %fusion.12, bf16[32,2,16,384]{3,2,1,0:T(8,128)(2,1)} %get-tuple-element.55), kind=kLoop, calls=%fused_computation.3 | loop fusion | flops 417792 | bytes 1671168 | tf_op jit(solution)/shard_map/concatenate | solution.py:375
  7.6 4.3 %collective-permute-start.3 = (bf16[34,2,16,384]{3,2,1,0:T(8,128)(2,1)S(1)}, bf16[34,2,16,384]{3,2,1,0:T(8,128)(2,1)}, u32[]{:S(2)}, u32[]{:S(2)}) collective-permute-start(bf16[34,2,16,384]{3,2,1,0:T(8,128)(2,1)S(1)} %pad_maximum_fusion.3), channel_id=1, source_target_pairs={{4,8},{12,16},{20,24},{28,32},{36,40},{44,48},{52,56},{60,64},{68,... | collective-permute-start | bytes 2506760 | tf_op jit(solution)/shard_map/ppermute | solution.py:380
  11.9 1.1 %fusion.13 = (bf16[1,1,64,2,384]{4,3,2,1,0:T(2,128)(2,1)S(1)}, bf16[1,1,64,2,384]{4,3,2,1,0:T(2,128)(2,1)S(1)}) fusion(bf16[2,32,64,2,384]{4,3,2,1,0:T(2,128)(2,1)} %refs_13_.1), kind=kLoop, calls=%fused_computation.47 | loop fusion | bytes 393216 | tf_op jit(solution)/shard_map/slice | solution.py:360
  13.3 1.1 %pad_maximum_fusion.1 = bf16[9,2,64,384]{3,2,1,0:T(8,128)(2,1)} fusion(bf16[1,2,64,384]{3,2,1,0:T(8,128)(2,1)S(1)} %get-tuple-element.70, bf16[8,2,64,384]{3,2,1,0:T(8,128)(2,1)S(1)} %get-tuple-element.59), kind=kLoop, calls=%fused_computation.1 | loop fusion | flops 442368 | bytes 1769472 | tf_op jit(solution)/shard_map/concatenate | solution.py:362
  14.4 1.1 %pad_maximum_fusion = bf16[9,2,64,384]{3,2,1,0:T(8,128)(2,1)} fusion(bf16[1,2,64,384]{3,2,1,0:T(8,128)(2,1)S(1)} %get-tuple-element.69, bf16[8,2,64,384]{3,2,1,0:T(8,128)(2,1)S(1)} %get-tuple-element.60), kind=kLoop, calls=%fused_computation | loop fusion | flops 442368 | bytes 1769472 | tf_op jit(solution)/shard_map/concatenate | solution.py:361
  15.5 1.3 %collective-permute-start = (bf16[9,2,64,384]{3,2,1,0:T(8,128)(2,1)}, bf16[9,2,64,384]{3,2,1,0:T(8,128)(2,1)S(1)}, u32[]{:S(2)}, u32[]{:S(2)}) collective-permute-start(bf16[9,2,64,384]{3,2,1,0:T(8,128)(2,1)} %pad_maximum_fusion), channel_id=1, source_target_pairs={{0,1},{1,2},{2,3},{4,5},{5,6},{6,7},{8,9},{9,10},{10,11},{12,13},{... | collective-permute-start | bytes 2654216 | tf_op jit(solution)/shard_map/ppermute | solution.py:26
  16.7 4.6 %collective-permute-start.1 = (bf16[9,2,64,384]{3,2,1,0:T(8,128)(2,1)}, bf16[9,2,64,384]{3,2,1,0:T(8,128)(2,1)S(1)}, u32[]{:S(2)}, u32[]{:S(2)}) collective-permute-start(bf16[9,2,64,384]{3,2,1,0:T(8,128)(2,1)} %pad_maximum_fusion.1), channel_id=1, source_target_pairs={{1,0},{2,1},{3,2},{5,4},{6,5},{7,6},{9,8},{10,9},{11,10},{13,12},{... | collective-permute-start | bytes 2654216 | tf_op jit(solution)/shard_map/ppermute | solution.py:26
  21.5 2.5 %wake_pack.1 = bf16[32,208,128]{2,1,0:T(8,128)(2,1)} custom-call(s32[1,512]{1,0:T(1,128)S(1)} %bitcast.65, s32[1,512]{1,0:T(1,128)S(1)} %bitcast.66, bf16[2,512,384]{2,1,0:T(8,128)(2,1)S(1)} %bitcast.64), custom_call_target="tpu_custom_call" | custom-call | tf_op jit(solution)/shard_map/wake_pack/pallas_call | solution.py:69
  24.0 7.4 %all-to-all-start = ((bf16[32,208,128]{2,1,0:T(8,128)(2,1)}), bf16[32,208,128]{2,1,0:T(8,128)(2,1)S(1)}, u32[]{:S(2)}, u32[]{:S(2)}) async-start(bf16[32,208,128]{2,1,0:T(8,128)(2,1)} %wake_pack.1), calls=%async_computation | async-start | bytes 3407872 | tf_op jit(solution)/shard_map/all_to_all | solution.py:389
  31.4 14.7 %surface_inside.1.refs_15_ = bf16[32,64,2,384]{3,2,1,0:T(2,128)(2,1)} custom-call(s32[4,4,8]{2,1,0:T(4,128)} %refs_0_.3, s32[1]{0:T(128)} %bitcast.refs_1_, bf16[32,2,64,384]{3,2,1,0:T(8,128)(2,1)} %bitcast.68, bf16[34,2,16,384]{3,2,1,0:T(8,128)(2,1)} %collective-permute-done.2.refs_3_.refs_5_, ...), custom_call_target="tpu_custom_call" | custom-call | flops 3249999872 | bytes 14000000 | tf_op jit(solution)/shard_map/surface_inside/pallas_call | solution.py:315
  46.3 1.0 %pad_maximum_fusion.5 = bf16[16,2,16,384]{3,2,1,0:T(8,128)(2,1)} fusion(bf16[8,2,16,384]{3,2,1,0:T(8,128)(2,1)S(1)} %get-tuple-element.63, bf16[8,2,16,384]{3,2,1,0:T(8,128)(2,1)S(1)} %get-tuple-element.61), kind=kLoop, calls=%fused_computation.8 | loop fusion | flops 196608 | bytes 786432 | tf_op jit(solution)/shard_map/concatenate | solution.py:397
  47.3 4.3 %collective-permute-start.5 = (bf16[16,2,16,384]{3,2,1,0:T(8,128)(2,1)}, bf16[16,2,16,384]{3,2,1,0:T(8,128)(2,1)}, u32[]{:S(2)}, u32[]{:S(2)}) collective-permute-start(bf16[16,2,16,384]{3,2,1,0:T(8,128)(2,1)} %pad_maximum_fusion.5), channel_id=1, source_target_pairs={{4,8},{12,16},{20,24},{28,32},{36,40},{44,48},{52,56},{60,64},{68,... | collective-permute-start | bytes 1179656 | tf_op jit(solution)/shard_map/ppermute | solution.py:403
  51.6 0.8 pad_maximum_fusion.4
  52.4 1.8 %all-to-all-done.got_ref = bf16[32,208,128]{2,1,0:T(8,128)(2,1)S(1)} async-done(((bf16[32,208,128]{2,1,0:T(8,128)(2,1)}), bf16[32,208,128]{2,1,0:T(8,128)(2,1)S(1)}, u32[]{:S(2)}, u32[]{:S(2)}) %all-to-all-start) | async-done | bytes 1703968 | tf_op jit(solution)/shard_map/all_to_all | solution.py:389
  54.7 1.3 %collective-permute-start.6 = (bf16[2,64,384]{2,1,0:T(8,128)(2,1)S(1)}, bf16[2,64,384]{2,1,0:T(8,128)(2,1)S(1)}, u32[]{:S(2)}, u32[]{:S(2)}) collective-permute-start(bf16[2,64,384]{2,1,0:T(8,128)(2,1)S(1)} %convert_element_type.84), channel_id=1, source_target_pairs={{1,0},{2,3},{5,4},{6,7},{9,8},{10,11},{13,12},{14,15},{17,16},{18,... | collective-permute-start | bytes 294920 | tf_op jit(solution)/shard_map/ppermute | solution.py:412
  56.0 2.8 %collective-permute-done.5.refs_8_ = bf16[16,2,16,384]{3,2,1,0:T(8,128)(2,1)} collective-permute-done((bf16[16,2,16,384]{3,2,1,0:T(8,128)(2,1)}, bf16[16,2,16,384]{3,2,1,0:T(8,128)(2,1)}, u32[]{:S(2)}, u32[]{:S(2)}) %collective-permute-start.5) | collective-permute-done | bytes 393248 | tf_op jit(solution)/shard_map/ppermute | solution.py:403
  58.8 16.3 %surface_rim.1 = bf16[32,64,2,384]{3,2,1,0:T(2,128)(2,1)} custom-call(s32[4,4,8]{2,1,0:T(4,128)} %refs_0_.3, s32[1]{0:T(128)} %bitcast.refs_1_, bf16[32,2,64,384]{3,2,1,0:T(8,128)(2,1)} %bitcast.69, bf16[9,2,64,384]{3,2,1,0:T(8,128)(2,1)} %copy-done.3, bf16[9,2,64,384]{3,2,1,0:T(8,128)(2,1)} %copy-done.4, ...), custom_call_target="tpu_custom_call", output_to_operand_aliasing={{}: (15, {})} | custom-call | flops 3249999872 | bytes 14000000 | tf_op jit(solution)/shard_map/surface_rim/pallas_call | solution.py:315
  75.1 2.1 %collective-permute-start.7 = (bf16[2,64,384]{2,1,0:T(8,128)(2,1)S(1)}, bf16[2,64,384]{2,1,0:T(8,128)(2,1)S(1)}, u32[]{:S(2)}, u32[]{:S(2)}) collective-permute-start(bf16[2,64,384]{2,1,0:T(8,128)(2,1)S(1)} %fusion.4), channel_id=1, source_target_pairs={{0,3},{3,0},{4,7},{7,4},{8,11},{11,8},{12,15},{15,12},{16,19},{19,... | collective-permute-start | bytes 294920 | tf_op jit(solution)/shard_map/ppermute | solution.py:414
  77.3 1.1 %fusion.14 = (bf16[1,64,2,384]{3,2,1,0:T(2,128)(2,1)S(1)}, bf16[1,64,2,384]{3,2,1,0:T(2,128)(2,1)S(1)}) fusion(bf16[32,64,2,384]{3,2,1,0:T(2,128)(2,1)} %surface_rim.1), kind=kLoop, calls=%fused_computation.48 | loop fusion | bytes 393216 | tf_op jit(solution)/shard_map/slice | solution.py:417
  78.3 4.5 %collective-permute-done.7 = bf16[2,64,384]{2,1,0:T(8,128)(2,1)S(1)} collective-permute-done((bf16[2,64,384]{2,1,0:T(8,128)(2,1)S(1)}, bf16[2,64,384]{2,1,0:T(8,128)(2,1)S(1)}, u32[]{:S(2)}, u32[]{:S(2)}) %collective-permute-start.7) | collective-permute-done | bytes 98336 | tf_op jit(solution)/shard_map/ppermute | solution.py:414
  (41 shorter events, 3.1 us)
Async XLA Ops:
  0.0 3.7 %copy-start.6 = (f32[2,32,64]{2,1,0:T(8,128)S(1)}, f32[2,32,64]{2,1,0:T(8,128)}, u32[]{:S(2)}) copy-start(f32[2,32,64]{2,1,0:T(8,128)} %refs_14_.1) | copy-start | bytes 49156
  2.6 10.5 %copy-start.2 = (bf16[32,64,2,384]{3,1,2,0:T(8,128)(2,1)}, bf16[32,64,2,384]{3,1,2,0:T(8,128)(2,1)S(1)}, u32[]{:S(2)}) copy-start(bf16[32,64,2,384]{3,1,2,0:T(8,128)(2,1)S(1)} %copy.68) | copy-start | bytes 9437188
  6.2 17.8 %collective-permute-start.2 = (bf16[34,2,16,384]{3,2,1,0:T(8,128)(2,1)}, bf16[34,2,16,384]{3,2,1,0:T(8,128)(2,1)}, u32[]{:S(2)}, u32[]{:S(2)}) collective-permute-start(bf16[34,2,16,384]{3,2,1,0:T(8,128)(2,1)} %pad_maximum_fusion.2), channel_id=1, source_target_pairs={{0,4},{4,0},{8,12},{12,8},{16,20},{20,16},{24,28},{28,24},{32,36},... | collective-permute-start | bytes 2506760 | tf_op jit(solution)/shard_map/ppermute | solution.py:379
  7.6 16.4 %collective-permute-start.3 = (bf16[34,2,16,384]{3,2,1,0:T(8,128)(2,1)S(1)}, bf16[34,2,16,384]{3,2,1,0:T(8,128)(2,1)}, u32[]{:S(2)}, u32[]{:S(2)}) collective-permute-start(bf16[34,2,16,384]{3,2,1,0:T(8,128)(2,1)S(1)} %pad_maximum_fusion.3), channel_id=1, source_target_pairs={{4,8},{12,16},{20,24},{28,32},{36,40},{44,48},{52,56},{60,64},{68,... | collective-permute-start | bytes 2506760 | tf_op jit(solution)/shard_map/ppermute | solution.py:380
  13.1 8.2 %copy-start.5 = (bf16[512,2,384]{2,1,0:T(2,128)(2,1)S(1)}, bf16[512,2,384]{2,1,0:T(2,128)(2,1)}, u32[]{:S(2)}) copy-start(bf16[512,2,384]{2,1,0:T(2,128)(2,1)} %param.17) | copy-start | bytes 2359300
  13.3 8.1 %copy-start = (s32[512,1]{0,1:T(1,128)S(1)}, s32[512,1]{0,1:T(1,128)}, u32[]{:S(2)}) copy-start(s32[512,1]{0,1:T(1,128)} %param.18) | copy-start | bytes 6148
  13.3 8.1 %copy-start.1 = (s32[512]{0:T(512)S(1)}, s32[512]{0:T(512)}, u32[]{:S(2)}) copy-start(s32[512]{0:T(512)} %param.19) | copy-start | bytes 6148
  15.5 30.7 %collective-permute-start = (bf16[9,2,64,384]{3,2,1,0:T(8,128)(2,1)}, bf16[9,2,64,384]{3,2,1,0:T(8,128)(2,1)S(1)}, u32[]{:S(2)}, u32[]{:S(2)}) collective-permute-start(bf16[9,2,64,384]{3,2,1,0:T(8,128)(2,1)} %pad_maximum_fusion), channel_id=1, source_target_pairs={{0,1},{1,2},{2,3},{4,5},{5,6},{6,7},{8,9},{9,10},{10,11},{12,13},{... | collective-permute-start | bytes 2654216 | tf_op jit(solution)/shard_map/ppermute | solution.py:26
  16.7 29.4 %collective-permute-start.1 = (bf16[9,2,64,384]{3,2,1,0:T(8,128)(2,1)}, bf16[9,2,64,384]{3,2,1,0:T(8,128)(2,1)S(1)}, u32[]{:S(2)}, u32[]{:S(2)}) collective-permute-start(bf16[9,2,64,384]{3,2,1,0:T(8,128)(2,1)} %pad_maximum_fusion.1), channel_id=1, source_target_pairs={{1,0},{2,1},{3,2},{5,4},{6,5},{7,6},{9,8},{10,9},{11,10},{13,12},{... | collective-permute-start | bytes 2654216 | tf_op jit(solution)/shard_map/ppermute | solution.py:26
  24.0 30.2 %all-to-all-start = ((bf16[32,208,128]{2,1,0:T(8,128)(2,1)}), bf16[32,208,128]{2,1,0:T(8,128)(2,1)S(1)}, u32[]{:S(2)}, u32[]{:S(2)}) async-start(bf16[32,208,128]{2,1,0:T(8,128)(2,1)} %wake_pack.1), calls=%async_computation | async-start | bytes 3407872 | tf_op jit(solution)/shard_map/all_to_all | solution.py:389
  46.1 12.7 %copy-start.3 = (bf16[9,2,64,384]{3,2,1,0:T(8,128)(2,1)}, bf16[9,2,64,384]{3,2,1,0:T(8,128)(2,1)S(1)}, u32[]{:S(2)}) copy-start(bf16[9,2,64,384]{3,2,1,0:T(8,128)(2,1)S(1)} %collective-permute-done.refs_3_) | copy-start | bytes 2654212
  46.1 12.6 %copy-start.4 = (bf16[9,2,64,384]{3,2,1,0:T(8,128)(2,1)}, bf16[9,2,64,384]{3,2,1,0:T(8,128)(2,1)S(1)}, u32[]{:S(2)}) copy-start(bf16[9,2,64,384]{3,2,1,0:T(8,128)(2,1)S(1)} %collective-permute-done.1.refs_4_) | copy-start | bytes 2654212
  47.3 11.5 %collective-permute-start.5 = (bf16[16,2,16,384]{3,2,1,0:T(8,128)(2,1)}, bf16[16,2,16,384]{3,2,1,0:T(8,128)(2,1)}, u32[]{:S(2)}, u32[]{:S(2)}) collective-permute-start(bf16[16,2,16,384]{3,2,1,0:T(8,128)(2,1)} %pad_maximum_fusion.5), channel_id=1, source_target_pairs={{4,8},{12,16},{20,24},{28,32},{36,40},{44,48},{52,56},{60,64},{68,... | collective-permute-start | bytes 1179656 | tf_op jit(solution)/shard_map/ppermute | solution.py:403
  52.4 6.4 %collective-permute-start.4 = (bf16[16,2,16,384]{3,2,1,0:T(8,128)(2,1)}, bf16[16,2,16,384]{3,2,1,0:T(8,128)(2,1)}, u32[]{:S(2)}, u32[]{:S(2)}) collective-permute-start(bf16[16,2,16,384]{3,2,1,0:T(8,128)(2,1)} %pad_maximum_fusion.4), channel_id=1, source_target_pairs={{0,4},{4,0},{8,12},{12,8},{16,20},{20,16},{24,28},{28,24},{32,36},... | collective-permute-start | bytes 1179656 | tf_op jit(solution)/shard_map/ppermute | solution.py:402
  54.7 20.4 %collective-permute-start.6 = (bf16[2,64,384]{2,1,0:T(8,128)(2,1)S(1)}, bf16[2,64,384]{2,1,0:T(8,128)(2,1)S(1)}, u32[]{:S(2)}, u32[]{:S(2)}) collective-permute-start(bf16[2,64,384]{2,1,0:T(8,128)(2,1)S(1)} %convert_element_type.84), channel_id=1, source_target_pairs={{1,0},{2,3},{5,4},{6,7},{9,8},{10,11},{13,12},{14,15},{17,16},{18,... | collective-permute-start | bytes 294920 | tf_op jit(solution)/shard_map/ppermute | solution.py:412
  75.1 7.7 %collective-permute-start.7 = (bf16[2,64,384]{2,1,0:T(8,128)(2,1)S(1)}, bf16[2,64,384]{2,1,0:T(8,128)(2,1)S(1)}, u32[]{:S(2)}, u32[]{:S(2)}) collective-permute-start(bf16[2,64,384]{2,1,0:T(8,128)(2,1)S(1)} %fusion.4), channel_id=1, source_target_pairs={{0,3},{3,0},{4,7},{7,4},{8,11},{11,8},{12,15},{15,12},{16,19},{19,... | collective-permute-start | bytes 294920 | tf_op jit(solution)/shard_map/ppermute | solution.py:414

commit v2 on v1

--- a/solution.py
+++ b/solution.py
@@ -137,7 +137,9 @@
     metric_ref,
     *rest,
 ):
-    out_ref, blocks, factors, stage, weights, spread, gradient, rim, chord_row, mixed = rest[-10:]
+    out_ref, blocks, factors, stage, weights, spread, gradient, rim, chord_row, mixed, near = (
+        rest[-11:]
+    )
     step = pl.program_id(0)
     c = pl.program_id(1)
     steps = pl.num_programs(0)
@@ -212,22 +214,17 @@
         return [stage[slot, pl.ds(part, cols, stride=2), :] * factor for part in range(2)]
 
     sources = [before_ref.at[0, 0]] + [down_ref.at[0, a] for a in range(BC)] + [after_ref.at[0, 0]]
-    for a, source in enumerate(sources):
-        pair = weighted(source, a, factors[0, a])
+    def weigh_row(a):
+        pair = weighted(sources[a], a, factors[0, a])
         for part in range(2):
-            weights[a, part] = pair[part].astype(BF16)
-
-    if not inside:
-
-        @pl.when(step == 0)
-        def _():
-            weights[0] = chord_row[0, c]
-
-        @pl.when(step == steps - 1)
-        def _():
-            weights[BC + 1] = chord_row[1, c]
-
-    for a in range(BC):
+            value = pair[part].astype(BF16)
+            if not inside and a == 0:
+                value = jnp.where(step == 0, chord_row[0, c, part], value)
+            if not inside and a == BC + 1:
+                value = jnp.where(step == steps - 1, chord_row[1, c, part], value)
+            weights[a, part] = value
+
+    def slope_row(a):
         pair = weighted(along_ref.at[0, a], BC + 2 + a, factors[1, a + 1])
         for part in range(2):
             line = spread.at[a, part]
@@ -238,9 +235,19 @@
             down = weights[a, part].astype(F32) - weights[a + 2, part].astype(F32)
             gradient[a, part] = 0.5 * (down + along)
 
+    work = [(weigh_row, a) for a in range(3)]
+    for a in range(BC):
+        work.append((slope_row, a))
+        if a + 3 < BC + 2:
+            work.append((weigh_row, a + 3))
+    slots = aic_ref.shape[2]
+    turns = bcols * slots
     for u in range(bcols):
         total = jnp.zeros((BC * BS, 2 * LANES), F32)
-        for k in range(aic_ref.shape[2]):
+        for k in range(slots):
+            turn = u * slots + k
+            for call, a in work[turn * len(work) // turns : (turn + 1) * len(work) // turns]:
+                call(a)
             code = codes_ref[t, u, k]
             r = t + code // 3
             q = u + code % 3
@@ -255,12 +262,13 @@
             )
             matrix = jnp.concatenate([aic_ref[0, u, k, 0], aic_ref[0, u, k, 1]], axis=1)
             total = total + jnp.dot(matrix, source, preferred_element_type=F32)
-        for a in range(BC):
+        near[u] = total
+    for a in range(BC):
+        for u in range(bcols):
             for part in range(2):
-                near = total[a * BS : (a + 1) * BS, part * LANES : (part + 1) * LANES]
+                value = near[u, a * BS : (a + 1) * BS, part * LANES : (part + 1) * LANES]
                 slope = gradient[a, part, u * BS : (u + 1) * BS, :]
-                mixed[a, pl.ds(2 * u * BS + part, BS, stride=2), :] = near + slope
-    for a in range(BC):
+                mixed[a, pl.ds(2 * u * BS + part, BS, stride=2), :] = value + slope
         out_ref.at[a].reshape(2 * cols, LANES)[...] = mixed[a].astype(BF16)
 
 
@@ -328,6 +336,7 @@
             pltpu.VMEM((R // LANES, 2, 2, rows, LANES), F32),
             pltpu.VMEM((2, R // LANES, 2, cols, LANES), BF16),
             pltpu.VMEM((BC, 2 * cols, LANES), F32),
+            pltpu.VMEM((bcols, BC * BS, 2 * LANES), F32),
         ],
         input_output_aliases=aliases,
         compiler_params=pltpu.CompilerParams(vmem_limit_bytes=56 * 1024 * 1024),

time: 85 us -> 84.6 us (level)
  no operation moved by 1% of the time
where the time goes in v2:
time: 84.6 us; the launch traced here: 84 us
  Pallas kernels  33.6 us (40%)
  starting transfers between devices  25.3 us (30%)
  local copies, waits for them, and re-layouts  9.2 us (11%)
  waiting for transfers between devices  9.14 us (11%)
  other arithmetic  6.51 us (8%)
    pallas_call x2, Pallas kernels, surface(): pl.pallas_call(kernel, grid=(brows // 2, R // LANES), in_specs=specs, out...  30.6 us
    all_to_all x1, starting transfers between devices, per_device(): got = lax.all_to_all(packed, 'span', 0, 0, tiled=True)  7.37 us
    ppermute x2, starting transfers between devices, shift(): return lax.ppermute(array, axis, pairs)  5.88 us
    ppermute x1, waiting for transfers between devices, per_device(): lax.ppermute(partial.astype(BF16), 'chord', swap).astype(F32)  4.51 us
    ppermute x1, starting transfers between devices, per_device(): outer = lax.ppermute(outer_send, 'span', outer_pairs)  4.32 us
    ppermute x1, starting transfers between devices, per_device(): outer_corner = lax.ppermute(corner(outer_col), 'span', outer_pairs)  4.31 us
    ppermute x1, waiting for transfers between devices, per_device(): outer_corner = lax.ppermute(corner(outer_col), 'span', outer_pairs)  2.8 us
    unnamed x17, local copies, waits for them, and re-layouts  2.65 us
  transfers between devices with their start and end apart: 9, of which 3 were waited for; matrix products, arithmetic and copies ran while one was open for 9% of the time, Pallas kernels for 40%

profile of v2, /device:TPU:56, one launch (start us, length us, event | category | flops | bytes accessed | tf_op | source)
XLA Modules:
  0.0 84.0 jit_solution(1038631166046778358)
XLA Ops:
  0.0 2.6 %copy.68 = bf16[32,64,2,384]{3,1,2,0:T(8,128)(2,1)S(1)} copy(bf16[32,64,2,384]{3,2,1,0:T(2,128)(2,1)} %param.12) | data formatting | bytes 6291456 | tf_op args[0]
  2.6 1.0 %constant_dynamic-slice_fusion.4 = (bf16[1,32,1,2,384]{4,3,2,1,0:T(2,128)(2,1)S(1)}, bf16[1,32,1,2,384]{4,3,2,1,0:T(2,128)(2,1)S(1)}) fusion(bf16[2,32,64,2,384]{4,3,2,1,0:T(2,128)(2,1)} %refs_13_.1, s32[]{:T(128)S(6)} %select_n.36, s32[]{:T(128)S(6)} %select_n.34), kind=kLoop, calls=%fused_computation.42 | loop fusion | bytes 196616 | tf_op jit(solution)/shard_map/dynamic_slice | solution.py:380
  4.0 1.1 %dynamic-slice_bitcast_fusion = (bf16[32,2,16,384]{3,2,1,0:T(8,128)(2,1)}, bf16[32,2,16,384]{3,2,1,0:T(8,128)(2,1)S(1)}) fusion(bf16[32,64,2,384]{3,1,2,0:T(8,128)(2,1)S(1)} %copy.68, s32[]{:T(128)S(6)} %select_n.35, s32[]{:T(128)S(6)} %select_n.33), kind=kLoop, calls=%fused_computation.5 | loop fusion | bytes 3145736 | tf_op jit(solution)/shard_map/dynamic_slice | solution.py:379
  5.2 1.0 %pad_maximum_fusion.2 = bf16[34,2,16,384]{3,2,1,0:T(8,128)(2,1)} fusion(bf16[2,2,16,384]{3,2,1,0:T(8,128)(2,1)S(1)} %fusion.11, bf16[32,2,16,384]{3,2,1,0:T(8,128)(2,1)S(1)} %get-tuple-element.56), kind=kLoop, calls=%fused_computation.2 | loop fusion | flops 417792 | bytes 1671168 | tf_op jit(solution)/shard_map/concatenate | solution.py:384
  6.3 1.2 %pad_maximum_fusion.3 = bf16[34,2,16,384]{3,2,1,0:T(8,128)(2,1)S(1)} fusion(bf16[2,2,16,384]{3,2,1,0:T(8,128)(2,1)S(1)} %fusion.12, bf16[32,2,16,384]{3,2,1,0:T(8,128)(2,1)} %get-tuple-element.55), kind=kLoop, calls=%fused_computation.3 | loop fusion | flops 417792 | bytes 1671168 | tf_op jit(solution)/shard_map/concatenate | solution.py:384
  7.6 4.3 %collective-permute-start.3 = (bf16[34,2,16,384]{3,2,1,0:T(8,128)(2,1)S(1)}, bf16[34,2,16,384]{3,2,1,0:T(8,128)(2,1)}, u32[]{:S(2)}, u32[]{:S(2)}) collective-permute-start(bf16[34,2,16,384]{3,2,1,0:T(8,128)(2,1)S(1)} %pad_maximum_fusion.3), channel_id=1, source_target_pairs={{4,8},{12,16},{20,24},{28,32},{36,40},{44,48},{52,56},{60,64},{68,... | collective-permute-start | bytes 2506760 | tf_op jit(solution)/shard_map/ppermute | solution.py:389
  11.9 1.1 %fusion.13 = (bf16[1,1,64,2,384]{4,3,2,1,0:T(2,128)(2,1)S(1)}, bf16[1,1,64,2,384]{4,3,2,1,0:T(2,128)(2,1)S(1)}) fusion(bf16[2,32,64,2,384]{4,3,2,1,0:T(2,128)(2,1)} %refs_13_.1), kind=kLoop, calls=%fused_computation.47 | loop fusion | bytes 393216 | tf_op jit(solution)/shard_map/slice | solution.py:369
  13.3 1.1 %pad_maximum_fusion.1 = bf16[9,2,64,384]{3,2,1,0:T(8,128)(2,1)} fusion(bf16[1,2,64,384]{3,2,1,0:T(8,128)(2,1)S(1)} %get-tuple-element.70, bf16[8,2,64,384]{3,2,1,0:T(8,128)(2,1)S(1)} %get-tuple-element.59), kind=kLoop, calls=%fused_computation.1 | loop fusion | flops 442368 | bytes 1769472 | tf_op jit(solution)/shard_map/concatenate | solution.py:371
  14.4 1.1 %pad_maximum_fusion = bf16[9,2,64,384]{3,2,1,0:T(8,128)(2,1)} fusion(bf16[1,2,64,384]{3,2,1,0:T(8,128)(2,1)S(1)} %get-tuple-element.69, bf16[8,2,64,384]{3,2,1,0:T(8,128)(2,1)S(1)} %get-tuple-element.60), kind=kLoop, calls=%fused_computation | loop fusion | flops 442368 | bytes 1769472 | tf_op jit(solution)/shard_map/concatenate | solution.py:370
  15.5 1.3 %collective-permute-start = (bf16[9,2,64,384]{3,2,1,0:T(8,128)(2,1)}, bf16[9,2,64,384]{3,2,1,0:T(8,128)(2,1)S(1)}, u32[]{:S(2)}, u32[]{:S(2)}) collective-permute-start(bf16[9,2,64,384]{3,2,1,0:T(8,128)(2,1)} %pad_maximum_fusion), channel_id=1, source_target_pairs={{0,1},{1,2},{2,3},{4,5},{5,6},{6,7},{8,9},{9,10},{10,11},{12,13},{... | collective-permute-start | bytes 2654216 | tf_op jit(solution)/shard_map/ppermute | solution.py:26
  16.7 4.6 %collective-permute-start.1 = (bf16[9,2,64,384]{3,2,1,0:T(8,128)(2,1)}, bf16[9,2,64,384]{3,2,1,0:T(8,128)(2,1)S(1)}, u32[]{:S(2)}, u32[]{:S(2)}) collective-permute-start(bf16[9,2,64,384]{3,2,1,0:T(8,128)(2,1)} %pad_maximum_fusion.1), channel_id=1, source_target_pairs={{1,0},{2,1},{3,2},{5,4},{6,5},{7,6},{9,8},{10,9},{11,10},{13,12},{... | collective-permute-start | bytes 2654216 | tf_op jit(solution)/shard_map/ppermute | solution.py:26
  21.5 2.5 %wake_pack.1 = bf16[32,208,128]{2,1,0:T(8,128)(2,1)} custom-call(s32[1,512]{1,0:T(1,128)S(1)} %bitcast.65, s32[1,512]{1,0:T(1,128)S(1)} %bitcast.66, bf16[2,512,384]{2,1,0:T(8,128)(2,1)S(1)} %bitcast.64), custom_call_target="tpu_custom_call" | custom-call | tf_op jit(solution)/shard_map/wake_pack/pallas_call | solution.py:69
  24.0 7.4 %all-to-all-start = ((bf16[32,208,128]{2,1,0:T(8,128)(2,1)}), bf16[32,208,128]{2,1,0:T(8,128)(2,1)S(1)}, u32[]{:S(2)}, u32[]{:S(2)}) async-start(bf16[32,208,128]{2,1,0:T(8,128)(2,1)} %wake_pack.1), calls=%async_computation | async-start | bytes 3407872 | tf_op jit(solution)/shard_map/all_to_all | solution.py:398
  31.4 14.7 %surface_inside.1.refs_15_ = bf16[32,64,2,384]{3,2,1,0:T(2,128)(2,1)} custom-call(s32[4,4,8]{2,1,0:T(4,128)} %refs_0_.3, s32[1]{0:T(128)} %bitcast.refs_1_, bf16[32,2,64,384]{3,2,1,0:T(8,128)(2,1)} %bitcast.68, bf16[34,2,16,384]{3,2,1,0:T(8,128)(2,1)} %collective-permute-done.2.refs_3_.refs_5_, ...), custom_call_target="tpu_custom_call" | custom-call | flops 3249999872 | bytes 14000000 | tf_op jit(solution)/shard_map/surface_inside/pallas_call | solution.py:323
  46.3 1.0 %pad_maximum_fusion.5 = bf16[16,2,16,384]{3,2,1,0:T(8,128)(2,1)} fusion(bf16[8,2,16,384]{3,2,1,0:T(8,128)(2,1)S(1)} %get-tuple-element.63, bf16[8,2,16,384]{3,2,1,0:T(8,128)(2,1)S(1)} %get-tuple-element.61), kind=kLoop, calls=%fused_computation.8 | loop fusion | flops 196608 | bytes 786432 | tf_op jit(solution)/shard_map/concatenate | solution.py:406
  47.3 4.3 %collective-permute-start.5 = (bf16[16,2,16,384]{3,2,1,0:T(8,128)(2,1)}, bf16[16,2,16,384]{3,2,1,0:T(8,128)(2,1)}, u32[]{:S(2)}, u32[]{:S(2)}) collective-permute-start(bf16[16,2,16,384]{3,2,1,0:T(8,128)(2,1)} %pad_maximum_fusion.5), channel_id=1, source_target_pairs={{4,8},{12,16},{20,24},{28,32},{36,40},{44,48},{52,56},{60,64},{68,... | collective-permute-start | bytes 1179656 | tf_op jit(solution)/shard_map/ppermute | solution.py:412
  51.6 0.8 pad_maximum_fusion.4
  52.4 1.8 %all-to-all-done.got_ref = bf16[32,208,128]{2,1,0:T(8,128)(2,1)S(1)} async-done(((bf16[32,208,128]{2,1,0:T(8,128)(2,1)}), bf16[32,208,128]{2,1,0:T(8,128)(2,1)S(1)}, u32[]{:S(2)}, u32[]{:S(2)}) %all-to-all-start) | async-done | bytes 1703968 | tf_op jit(solution)/shard_map/all_to_all | solution.py:398
  54.7 1.3 %collective-permute-start.6 = (bf16[2,64,384]{2,1,0:T(8,128)(2,1)S(1)}, bf16[2,64,384]{2,1,0:T(8,128)(2,1)S(1)}, u32[]{:S(2)}, u32[]{:S(2)}) collective-permute-start(bf16[2,64,384]{2,1,0:T(8,128)(2,1)S(1)} %convert_element_type.84), channel_id=1, source_target_pairs={{1,0},{2,3},{5,4},{6,7},{9,8},{10,11},{13,12},{14,15},{17,16},{18,... | collective-permute-start | bytes 294920 | tf_op jit(solution)/shard_map/ppermute | solution.py:421
  56.0 2.8 %collective-permute-done.5.refs_8_ = bf16[16,2,16,384]{3,2,1,0:T(8,128)(2,1)} collective-permute-done((bf16[16,2,16,384]{3,2,1,0:T(8,128)(2,1)}, bf16[16,2,16,384]{3,2,1,0:T(8,128)(2,1)}, u32[]{:S(2)}, u32[]{:S(2)}) %collective-permute-start.5) | collective-permute-done | bytes 393248 | tf_op jit(solution)/shard_map/ppermute | solution.py:412
  58.8 15.9 %surface_rim.1 = bf16[32,64,2,384]{3,2,1,0:T(2,128)(2,1)} custom-call(s32[4,4,8]{2,1,0:T(4,128)} %refs_0_.3, s32[1]{0:T(128)} %bitcast.refs_1_, bf16[32,2,64,384]{3,2,1,0:T(8,128)(2,1)} %bitcast.69, bf16[9,2,64,384]{3,2,1,0:T(8,128)(2,1)} %copy-done.3, bf16[9,2,64,384]{3,2,1,0:T(8,128)(2,1)} %copy-done.4, ...), custom_call_target="tpu_custom_call", output_to_operand_aliasing={{}: (15, {})} | custom-call | flops 3249999872 | bytes 14000000 | tf_op jit(solution)/shard_map/surface_rim/pallas_call | solution.py:323
  74.7 2.1 %collective-permute-start.7 = (bf16[2,64,384]{2,1,0:T(8,128)(2,1)S(1)}, bf16[2,64,384]{2,1,0:T(8,128)(2,1)S(1)}, u32[]{:S(2)}, u32[]{:S(2)}) collective-permute-start(bf16[2,64,384]{2,1,0:T(8,128)(2,1)S(1)} %fusion.4), channel_id=1, source_target_pairs={{0,3},{3,0},{4,7},{7,4},{8,11},{11,8},{12,15},{15,12},{16,19},{19,... | collective-permute-start | bytes 294920 | tf_op jit(solution)/shard_map/ppermute | solution.py:423
  76.9 1.1 %fusion.14 = (bf16[1,64,2,384]{3,2,1,0:T(2,128)(2,1)S(1)}, bf16[1,64,2,384]{3,2,1,0:T(2,128)(2,1)S(1)}) fusion(bf16[32,64,2,384]{3,2,1,0:T(2,128)(2,1)} %surface_rim.1), kind=kLoop, calls=%fused_computation.48 | loop fusion | bytes 393216 | tf_op jit(solution)/shard_map/slice | solution.py:426
  77.9 4.5 %collective-permute-done.7 = bf16[2,64,384]{2,1,0:T(8,128)(2,1)S(1)} collective-permute-done((bf16[2,64,384]{2,1,0:T(8,128)(2,1)S(1)}, bf16[2,64,384]{2,1,0:T(8,128)(2,1)S(1)}, u32[]{:S(2)}, u32[]{:S(2)}) %collective-permute-start.7) | collective-permute-done | bytes 98336 | tf_op jit(solution)/shard_map/ppermute | solution.py:423
  (41 shorter events, 3.1 us)
Async XLA Ops:
  0.0 3.7 %copy-start.6 = (f32[2,32,64]{2,1,0:T(8,128)S(1)}, f32[2,32,64]{2,1,0:T(8,128)}, u32[]{:S(2)}) copy-start(f32[2,32,64]{2,1,0:T(8,128)} %refs_14_.1) | copy-start | bytes 49156
  2.6 10.5 %copy-start.2 = (bf16[32,64,2,384]{3,1,2,0:T(8,128)(2,1)}, bf16[32,64,2,384]{3,1,2,0:T(8,128)(2,1)S(1)}, u32[]{:S(2)}) copy-start(bf16[32,64,2,384]{3,1,2,0:T(8,128)(2,1)S(1)} %copy.68) | copy-start | bytes 9437188
  6.2 17.8 %collective-permute-start.2 = (bf16[34,2,16,384]{3,2,1,0:T(8,128)(2,1)}, bf16[34,2,16,384]{3,2,1,0:T(8,128)(2,1)}, u32[]{:S(2)}, u32[]{:S(2)}) collective-permute-start(bf16[34,2,16,384]{3,2,1,0:T(8,128)(2,1)} %pad_maximum_fusion.2), channel_id=1, source_target_pairs={{0,4},{4,0},{8,12},{12,8},{16,20},{20,16},{24,28},{28,24},{32,36},... | collective-permute-start | bytes 2506760 | tf_op jit(solution)/shard_map/ppermute | solution.py:388
  7.6 16.4 %collective-permute-start.3 = (bf16[34,2,16,384]{3,2,1,0:T(8,128)(2,1)S(1)}, bf16[34,2,16,384]{3,2,1,0:T(8,128)(2,1)}, u32[]{:S(2)}, u32[]{:S(2)}) collective-permute-start(bf16[34,2,16,384]{3,2,1,0:T(8,128)(2,1)S(1)} %pad_maximum_fusion.3), channel_id=1, source_target_pairs={{4,8},{12,16},{20,24},{28,32},{36,40},{44,48},{52,56},{60,64},{68,... | collective-permute-start | bytes 2506760 | tf_op jit(solution)/shard_map/ppermute | solution.py:389
  13.1 8.2 %copy-start.5 = (bf16[512,2,384]{2,1,0:T(2,128)(2,1)S(1)}, bf16[512,2,384]{2,1,0:T(2,128)(2,1)}, u32[]{:S(2)}) copy-start(bf16[512,2,384]{2,1,0:T(2,128)(2,1)} %param.17) | copy-start | bytes 2359300
  13.3 8.1 %copy-start = (s32[512,1]{0,1:T(1,128)S(1)}, s32[512,1]{0,1:T(1,128)}, u32[]{:S(2)}) copy-start(s32[512,1]{0,1:T(1,128)} %param.18) | copy-start | bytes 6148
  13.3 8.1 %copy-start.1 = (s32[512]{0:T(512)S(1)}, s32[512]{0:T(512)}, u32[]{:S(2)}) copy-start(s32[512]{0:T(512)} %param.19) | copy-start | bytes 6148
  15.5 30.6 %collective-permute-start = (bf16[9,2,64,384]{3,2,1,0:T(8,128)(2,1)}, bf16[9,2,64,384]{3,2,1,0:T(8,128)(2,1)S(1)}, u32[]{:S(2)}, u32[]{:S(2)}) collective-permute-start(bf16[9,2,64,384]{3,2,1,0:T(8,128)(2,1)} %pad_maximum_fusion), channel_id=1, source_target_pairs={{0,1},{1,2},{2,3},{4,5},{5,6},{6,7},{8,9},{9,10},{10,11},{12,13},{... | collective-permute-start | bytes 2654216 | tf_op jit(solution)/shard_map/ppermute | solution.py:26
  16.7 29.4 %collective-permute-start.1 = (bf16[9,2,64,384]{3,2,1,0:T(8,128)(2,1)}, bf16[9,2,64,384]{3,2,1,0:T(8,128)(2,1)S(1)}, u32[]{:S(2)}, u32[]{:S(2)}) collective-permute-start(bf16[9,2,64,384]{3,2,1,0:T(8,128)(2,1)} %pad_maximum_fusion.1), channel_id=1, source_target_pairs={{1,0},{2,1},{3,2},{5,4},{6,5},{7,6},{9,8},{10,9},{11,10},{13,12},{... | collective-permute-start | bytes 2654216 | tf_op jit(solution)/shard_map/ppermute | solution.py:26
  24.0 30.2 %all-to-all-start = ((bf16[32,208,128]{2,1,0:T(8,128)(2,1)}), bf16[32,208,128]{2,1,0:T(8,128)(2,1)S(1)}, u32[]{:S(2)}, u32[]{:S(2)}) async-start(bf16[32,208,128]{2,1,0:T(8,128)(2,1)} %wake_pack.1), calls=%async_computation | async-start | bytes 3407872 | tf_op jit(solution)/shard_map/all_to_all | solution.py:398
  46.1 12.7 %copy-start.3 = (bf16[9,2,64,384]{3,2,1,0:T(8,128)(2,1)}, bf16[9,2,64,384]{3,2,1,0:T(8,128)(2,1)S(1)}, u32[]{:S(2)}) copy-start(bf16[9,2,64,384]{3,2,1,0:T(8,128)(2,1)S(1)} %collective-permute-done.refs_3_) | copy-start | bytes 2654212
  46.1 12.6 %copy-start.4 = (bf16[9,2,64,384]{3,2,1,0:T(8,128)(2,1)}, bf16[9,2,64,384]{3,2,1,0:T(8,128)(2,1)S(1)}, u32[]{:S(2)}) copy-start(bf16[9,2,64,384]{3,2,1,0:T(8,128)(2,1)S(1)} %collective-permute-done.1.refs_4_) | copy-start | bytes 2654212
  47.3 11.5 %collective-permute-start.5 = (bf16[16,2,16,384]{3,2,1,0:T(8,128)(2,1)}, bf16[16,2,16,384]{3,2,1,0:T(8,128)(2,1)}, u32[]{:S(2)}, u32[]{:S(2)}) collective-permute-start(bf16[16,2,16,384]{3,2,1,0:T(8,128)(2,1)} %pad_maximum_fusion.5), channel_id=1, source_target_pairs={{4,8},{12,16},{20,24},{28,32},{36,40},{44,48},{52,56},{60,64},{68,... | collective-permute-start | bytes 1179656 | tf_op jit(solution)/shard_map/ppermute | solution.py:412
  52.4 6.4 %collective-permute-start.4 = (bf16[16,2,16,384]{3,2,1,0:T(8,128)(2,1)}, bf16[16,2,16,384]{3,2,1,0:T(8,128)(2,1)}, u32[]{:S(2)}, u32[]{:S(2)}) collective-permute-start(bf16[16,2,16,384]{3,2,1,0:T(8,128)(2,1)} %pad_maximum_fusion.4), channel_id=1, source_target_pairs={{0,4},{4,0},{8,12},{12,8},{16,20},{20,16},{24,28},{28,24},{32,36},... | collective-permute-start | bytes 1179656 | tf_op jit(solution)/shard_map/ppermute | solution.py:411
  54.7 20.0 %collective-permute-start.6 = (bf16[2,64,384]{2,1,0:T(8,128)(2,1)S(1)}, bf16[2,64,384]{2,1,0:T(8,128)(2,1)S(1)}, u32[]{:S(2)}, u32[]{:S(2)}) collective-permute-start(bf16[2,64,384]{2,1,0:T(8,128)(2,1)S(1)} %convert_element_type.84), channel_id=1, source_target_pairs={{1,0},{2,3},{5,4},{6,7},{9,8},{10,11},{13,12},{14,15},{17,16},{18,... | collective-permute-start | bytes 294920 | tf_op jit(solution)/shard_map/ppermute | solution.py:421
  74.7 7.7 %collective-permute-start.7 = (bf16[2,64,384]{2,1,0:T(8,128)(2,1)S(1)}, bf16[2,64,384]{2,1,0:T(8,128)(2,1)S(1)}, u32[]{:S(2)}, u32[]{:S(2)}) collective-permute-start(bf16[2,64,384]{2,1,0:T(8,128)(2,1)S(1)} %fusion.4), channel_id=1, source_target_pairs={{0,3},{3,0},{4,7},{7,4},{8,11},{11,8},{12,15},{15,12},{16,19},{19,... | collective-permute-start | bytes 294920 | tf_op jit(solution)/shard_map/ppermute | solution.py:423

commit v3 on v2

--- a/solution.py
+++ b/solution.py
@@ -410,20 +410,21 @@
 
     inner_corner = lax.ppermute(corner(inner_col), "span", inner_pairs)
     outer_corner = lax.ppermute(corner(outer_col), "span", outer_pairs)
-    halos = (low, high, inner, outer, inner_corner, outer_corner)
-    out = surface(False, block_codes, place, own, halos, *shared, done=out)
-
     partial = sum_stations(got, cols)
     count = lax.axis_size("chord")
-    place = lax.axis_index("chord")
+    row = lax.axis_index("chord")
     half = count // 2
     pairs = [(i, 0 if i < half else count - 1) for i in (1, count - 2)]
     partial = partial + lax.ppermute(partial.astype(BF16), "chord", pairs).astype(F32)
     swap = [(0, count - 1), (count - 1, 0)]
     shed = partial + lax.ppermute(partial.astype(BF16), "chord", swap).astype(F32)
     shed = split_parts(shed)
-    first = out[0].astype(F32) - jnp.where(place == 0, 1.0, 0.0) * shed
-    last = out[rows - 1].astype(F32) + jnp.where(place == count - 1, 1.0, 0.0) * shed
+    shed, inner_corner = lax.optimization_barrier((shed, inner_corner))
+    halos = (low, high, inner, outer, inner_corner, outer_corner)
+    out = surface(False, block_codes, place, own, halos, *shared, done=out)
+
+    first = out[0].astype(F32) - jnp.where(row == 0, 1.0, 0.0) * shed
+    last = out[rows - 1].astype(F32) + jnp.where(row == count - 1, 1.0, 0.0) * shed
     return out.at[0].set(first.astype(BF16)).at[rows - 1].set(last.astype(BF16))
 
 

time: 84.6 us -> 99.5 us (1.18)
  the two profiles are of different devices: /device:TPU:56 before, /device:TPU:2 now
where the time goes in v3:
time: 99.5 us; the launch traced here: 98.8 us
  Pallas kernels  33.6 us (34%)
  starting transfers between devices  24.4 us (25%)
  waiting for transfers between devices  20.7 us (21%)
  local copies, waits for them, and re-layouts  12.1 us (12%)
  other arithmetic  7.84 us (8%)
    pallas_call x2, Pallas kernels, surface(): pl.pallas_call(kernel, grid=(brows // 2, R // LANES), in_specs=specs, out...  30.7 us
    all_to_all x1, starting transfers between devices, per_device(): got = lax.all_to_all(packed, 'span', 0, 0, tiled=True)  10.3 us
    unnamed x23, local copies, waits for them, and re-layouts  7.91 us
    ppermute x2, waiting for transfers between devices, shift(): return lax.ppermute(array, axis, pairs)  7.45 us
    ppermute x1, waiting for transfers between devices, per_device(): outer = lax.ppermute(outer_send, 'span', outer_pairs)  5.3 us
    ppermute x2, starting transfers between devices, shift(): return lax.ppermute(array, axis, pairs)  4.83 us
    ppermute x1, waiting for transfers between devices, per_device(): lax.ppermute(partial.astype(BF16), 'chord', swap).astype(F32)  4.56 us
    ppermute x1, waiting for transfers between devices, per_device(): lax.ppermute(partial.astype(BF16), 'chord', pairs).astype(F32)  3.36 us
  transfers between devices with their start and end apart: 9, of which 5 were waited for; matrix products, arithmetic and copies ran while one was open for 7% of the time, Pallas kernels for 18%

profile of v3, /device:TPU:2, one launch (start us, length us, event | category | flops | bytes accessed | tf_op | source)
XLA Modules:
  0.0 98.8 jit_solution(13226124856484504388)
XLA Ops:
  0.0 2.6 %copy.61 = bf16[32,64,2,384]{3,1,2,0:T(8,128)(2,1)S(1)} copy(bf16[32,64,2,384]{3,2,1,0:T(2,128)(2,1)} %param.12) | data formatting | bytes 6291456 | tf_op args[0]
  4.0 1.2 %dynamic-slice_bitcast_fusion = (bf16[32,2,16,384]{3,2,1,0:T(8,128)(2,1)}, bf16[32,2,16,384]{3,2,1,0:T(8,128)(2,1)S(1)}) fusion(bf16[32,64,2,384]{3,1,2,0:T(8,128)(2,1)S(1)} %copy.61, s32[]{:T(128)S(6)} %select_n.35, s32[]{:T(128)S(6)} %select_n.33), kind=kLoop, calls=%fused_computation.5 | loop fusion | bytes 3145736 | tf_op jit(solution)/shard_map/dynamic_slice | solution.py:379
  6.4 1.2 %pad_maximum_fusion.3 = bf16[34,2,16,384]{3,2,1,0:T(8,128)(2,1)S(1)} fusion(bf16[2,2,16,384]{3,2,1,0:T(8,128)(2,1)S(1)} %fusion.14, bf16[32,2,16,384]{3,2,1,0:T(8,128)(2,1)} %get-tuple-element.57), kind=kLoop, calls=%fused_computation.3 | loop fusion | flops 417792 | bytes 1671168 | tf_op jit(solution)/shard_map/concatenate | solution.py:384
  7.6 2.5 %collective-permute-start.3 = (bf16[34,2,16,384]{3,2,1,0:T(8,128)(2,1)S(1)}, bf16[34,2,16,384]{3,2,1,0:T(8,128)(2,1)}, u32[]{:S(2)}, u32[]{:S(2)}) collective-permute-start(bf16[34,2,16,384]{3,2,1,0:T(8,128)(2,1)S(1)} %pad_maximum_fusion.3), channel_id=1, source_target_pairs={{4,8},{12,16},{20,24},{28,32},{36,40},{44,48},{52,56},{60,64},{68,... | collective-permute-start | bytes 2506760 | tf_op jit(solution)/shard_map/ppermute | solution.py:389
  10.1 1.1 %fusion.15 = (bf16[1,1,64,2,384]{4,3,2,1,0:T(2,128)(2,1)S(1)}, bf16[1,1,64,2,384]{4,3,2,1,0:T(2,128)(2,1)S(1)}) fusion(bf16[2,32,64,2,384]{4,3,2,1,0:T(2,128)(2,1)} %refs_13_.1), kind=kLoop, calls=%fused_computation.48 | loop fusion | bytes 393216 | tf_op jit(solution)/shard_map/slice | solution.py:369
  11.5 1.1 %pad_maximum_fusion = bf16[9,2,64,384]{3,2,1,0:T(8,128)(2,1)} fusion(bf16[1,2,64,384]{3,2,1,0:T(8,128)(2,1)S(1)} %get-tuple-element.69, bf16[8,2,64,384]{3,2,1,0:T(8,128)(2,1)S(1)} %get-tuple-element.62), kind=kLoop, calls=%fused_computation | loop fusion | flops 442368 | bytes 1769472 | tf_op jit(solution)/shard_map/concatenate | solution.py:370
  12.6 1.0 %pad_maximum_fusion.1 = bf16[9,2,64,384]{3,2,1,0:T(8,128)(2,1)} fusion(bf16[1,2,64,384]{3,2,1,0:T(8,128)(2,1)S(1)} %get-tuple-element.70, bf16[8,2,64,384]{3,2,1,0:T(8,128)(2,1)S(1)} %get-tuple-element.61), kind=kLoop, calls=%fused_computation.1 | loop fusion | flops 442368 | bytes 1769472 | tf_op jit(solution)/shard_map/concatenate | solution.py:371
  13.7 2.5 %wake_pack.1 = bf16[32,208,128]{2,1,0:T(8,128)(2,1)} custom-call(s32[1,512]{1,0:T(1,128)S(1)} %bitcast.61, s32[1,512]{1,0:T(1,128)S(1)} %bitcast.62, bf16[2,512,384]{2,1,0:T(8,128)(2,1)S(1)} %bitcast.60), custom_call_target="tpu_custom_call" | custom-call | tf_op jit(solution)/shard_map/wake_pack/pallas_call | solution.py:69
  16.2 5.3 %collective-permute-done.3.refs_4_.refs_6_ = bf16[34,2,16,384]{3,2,1,0:T(8,128)(2,1)} collective-permute-done((bf16[34,2,16,384]{3,2,1,0:T(8,128)(2,1)S(1)}, bf16[34,2,16,384]{3,2,1,0:T(8,128)(2,1)}, u32[]{:S(2)}, u32[]{:S(2)}) %collective-permute-start.3) | collective-permute-done | bytes 835616 | tf_op jit(solution)/shard_map/ppermute | solution.py:389
  21.5 10.3 %all-to-all-start = ((bf16[32,208,128]{2,1,0:T(8,128)(2,1)}), bf16[32,208,128]{2,1,0:T(8,128)(2,1)S(1)}, u32[]{:S(2)}, u32[]{:S(2)}) async-start(bf16[32,208,128]{2,1,0:T(8,128)(2,1)} %wake_pack.1), calls=%async_computation | async-start | bytes 3407872 | tf_op jit(solution)/shard_map/all_to_all | solution.py:398
  31.8 3.5 %collective-permute-start = (bf16[9,2,64,384]{3,2,1,0:T(8,128)(2,1)}, bf16[9,2,64,384]{3,2,1,0:T(8,128)(2,1)S(1)}, u32[]{:S(2)}, u32[]{:S(2)}) collective-permute-start(bf16[9,2,64,384]{3,2,1,0:T(8,128)(2,1)} %pad_maximum_fusion), channel_id=1, source_target_pairs={{0,1},{1,2},{2,3},{4,5},{5,6},{6,7},{8,9},{9,10},{10,11},{12,13},{... | collective-permute-start | bytes 2654216 | tf_op jit(solution)/shard_map/ppermute | solution.py:26
  35.3 1.3 %collective-permute-start.1 = (bf16[9,2,64,384]{3,2,1,0:T(8,128)(2,1)}, bf16[9,2,64,384]{3,2,1,0:T(8,128)(2,1)S(1)}, u32[]{:S(2)}, u32[]{:S(2)}) collective-permute-start(bf16[9,2,64,384]{3,2,1,0:T(8,128)(2,1)} %pad_maximum_fusion.1), channel_id=1, source_target_pairs={{1,0},{2,1},{3,2},{5,4},{6,5},{7,6},{9,8},{10,9},{11,10},{13,12},{... | collective-permute-start | bytes 2654216 | tf_op jit(solution)/shard_map/ppermute | solution.py:26
  36.6 14.8 %surface_inside.1.refs_15_ = bf16[32,64,2,384]{3,2,1,0:T(2,128)(2,1)} custom-call(s32[4,4,8]{2,1,0:T(4,128)} %refs_0_.3, s32[1]{0:T(128)} %bitcast.refs_1_, bf16[32,2,64,384]{3,2,1,0:T(8,128)(2,1)} %bitcast.64, bf16[34,2,16,384]{3,2,1,0:T(8,128)(2,1)} %collective-permute-done.2.refs_3_.refs_5_, ...), custom_call_target="tpu_custom_call" | custom-call | flops 3249999872 | bytes 14000000 | tf_op jit(solution)/shard_map/surface_inside/pallas_call | solution.py:323
  51.4 3.4 %collective-permute-done.refs_3_ = bf16[9,2,64,384]{3,2,1,0:T(8,128)(2,1)S(1)} collective-permute-done((bf16[9,2,64,384]{3,2,1,0:T(8,128)(2,1)}, bf16[9,2,64,384]{3,2,1,0:T(8,128)(2,1)S(1)}, u32[]{:S(2)}, u32[]{:S(2)}) %collective-permute-start) | collective-permute-done | bytes 884768 | tf_op jit(solution)/shard_map/ppermute | solution.py:26
  54.8 4.1 %collective-permute-done.1.refs_4_ = bf16[9,2,64,384]{3,2,1,0:T(8,128)(2,1)S(1)} collective-permute-done((bf16[9,2,64,384]{3,2,1,0:T(8,128)(2,1)}, bf16[9,2,64,384]{3,2,1,0:T(8,128)(2,1)S(1)}, u32[]{:S(2)}, u32[]{:S(2)}) %collective-permute-start.1) | collective-permute-done | bytes 884768 | tf_op jit(solution)/shard_map/ppermute | solution.py:26
  60.6 1.3 %collective-permute-start.4 = (bf16[2,64,384]{2,0,1:T(2,128)(2,1)S(1)}, bf16[2,64,384]{2,0,1:T(2,128)(2,1)S(1)}, u32[]{:S(2)}, u32[]{:S(2)}) collective-permute-start(bf16[2,64,384]{2,0,1:T(2,128)(2,1)S(1)} %copy.58), channel_id=1, source_target_pairs={{1,0},{2,3},{5,4},{6,7},{9,8},{10,11},{13,12},{14,15},{17,16},{18,... | collective-permute-start | bytes 294920 | tf_op jit(solution)/shard_map/ppermute | solution.py:418
  62.0 2.4 %collective-permute-start.7 = (bf16[16,2,16,384]{3,2,1,0:T(8,128)(2,1)S(1)}, bf16[16,2,16,384]{3,2,1,0:T(8,128)(2,1)S(1)}, u32[]{:S(2)}, u32[]{:S(2)}) collective-permute-start(bf16[16,2,16,384]{3,2,1,0:T(8,128)(2,1)S(1)} %pad_maximum_fusion.5), channel_id=1, source_target_pairs={{4,8},{12,16},{20,24},{28,32},{36,40},{44,48},{52,56},{60,64},{68,... | collective-permute-start | bytes 1179656 | tf_op jit(solution)/shard_map/ppermute | solution.py:412
  64.3 3.4 %collective-permute-done.4 = bf16[2,64,384]{2,0,1:T(2,128)(2,1)S(1)} collective-permute-done((bf16[2,64,384]{2,0,1:T(2,128)(2,1)S(1)}, bf16[2,64,384]{2,0,1:T(2,128)(2,1)S(1)}, u32[]{:S(2)}, u32[]{:S(2)}) %collective-permute-start.4) | collective-permute-done | bytes 98336 | tf_op jit(solution)/shard_map/ppermute | solution.py:418
  67.9 3.1 %collective-permute-start.5 = (bf16[2,64,384]{2,0,1:T(2,128)(2,1)S(1)}, bf16[2,64,384]{2,0,1:T(2,128)(2,1)S(1)}, u32[]{:S(2)}, u32[]{:S(2)}) collective-permute-start(bf16[2,64,384]{2,0,1:T(2,128)(2,1)S(1)} %fusion.12), channel_id=1, source_target_pairs={{0,3},{3,0},{4,7},{7,4},{8,11},{11,8},{12,15},{15,12},{16,19},{19,... | collective-permute-start | bytes 294920 | tf_op jit(solution)/shard_map/ppermute | solution.py:420
  71.1 4.6 %collective-permute-done.5 = bf16[2,64,384]{2,0,1:T(2,128)(2,1)S(1)} collective-permute-done((bf16[2,64,384]{2,0,1:T(2,128)(2,1)S(1)}, bf16[2,64,384]{2,0,1:T(2,128)(2,1)S(1)}, u32[]{:S(2)}, u32[]{:S(2)}) %collective-permute-start.5) | collective-permute-done | bytes 98336 | tf_op jit(solution)/shard_map/ppermute | solution.py:420
  76.6 15.9 %surface_rim.1 = bf16[32,64,2,384]{3,2,1,0:T(2,128)(2,1)} custom-call(s32[4,4,8]{2,1,0:T(4,128)} %refs_0_.3, s32[1]{0:T(128)} %bitcast.refs_1_, bf16[32,2,64,384]{3,2,1,0:T(8,128)(2,1)} %bitcast.65, bf16[9,2,64,384]{3,2,1,0:T(8,128)(2,1)} %copy-done.4, bf16[9,2,64,384]{3,2,1,0:T(8,128)(2,1)} %copy-done.5, ...), custom_call_target="tpu_custom_call", output_to_operand_aliasing={{}: (15, {})} | custom-call | flops 3249999872 | bytes 14000000 | tf_op jit(solution)/shard_map/surface_rim/pallas_call | solution.py:323
  92.5 1.9 %copy.63 = bf16[32,64,2,384]{3,2,1,0:T(2,128)(2,1)S(1)} copy(bf16[32,64,2,384]{3,2,1,0:T(2,128)(2,1)} %surface_rim.1) | data formatting | bytes 6291456
  95.5 1.7 %copy-done.3 = bf16[32,64,2,384]{3,2,1,0:T(2,128)(2,1)} copy-done((bf16[32,64,2,384]{3,2,1,0:T(2,128)(2,1)}, bf16[32,64,2,384]{3,2,1,0:T(2,128)(2,1)S(1)}, u32[]{:S(2)}) %copy-start.3) | copy-done | bytes 3145752
  97.2 1.6 %fusion.9 = bf16[32,64,2,384]{3,2,1,0:T(2,128)(2,1)} fusion(bf16[32,64,2,384]{3,2,1,0:T(2,128)(2,1)} %copy-done.3, f32[64,2,384]{2,1,0:T(2,128)S(1)} %add_bitcast_fusion, bf16[32,64,2,384]{3,2,1,0:T(2,128)(2,1)} %surface_rim.1, f32[]{:T(128)S(6)} %select_n.38), kind=kLoop, calls=%fused_computation.25 | loop fusion | flops 196608 | bytes 393220 | tf_op jit(solution)/shard_map/scatter | solution.py:428
  (46 shorter events, 7.0 us)
Async XLA Ops:
  0.0 2.6 %copy-start.8 = (f32[2,32,64]{2,1,0:T(8,128)S(1)}, f32[2,32,64]{2,1,0:T(8,128)}, u32[]{:S(2)}) copy-start(f32[2,32,64]{2,1,0:T(8,128)} %refs_14_.1) | copy-start | bytes 49156
  2.6 8.7 %copy-start.2 = (bf16[32,64,2,384]{3,1,2,0:T(8,128)(2,1)}, bf16[32,64,2,384]{3,1,2,0:T(8,128)(2,1)S(1)}, u32[]{:S(2)}) copy-start(bf16[32,64,2,384]{3,1,2,0:T(8,128)(2,1)S(1)} %copy.61) | copy-start | bytes 9437188
  6.2 10.1 %collective-permute-start.2 = (bf16[34,2,16,384]{3,2,1,0:T(8,128)(2,1)}, bf16[34,2,16,384]{3,2,1,0:T(8,128)(2,1)}, u32[]{:S(2)}, u32[]{:S(2)}) collective-permute-start(bf16[34,2,16,384]{3,2,1,0:T(8,128)(2,1)} %pad_maximum_fusion.2), channel_id=1, source_target_pairs={{0,4},{4,0},{8,12},{12,8},{16,20},{20,16},{24,28},{28,24},{32,36},... | collective-permute-start | bytes 2506760 | tf_op jit(solution)/shard_map/ppermute | solution.py:388
  7.6 13.9 %collective-permute-start.3 = (bf16[34,2,16,384]{3,2,1,0:T(8,128)(2,1)S(1)}, bf16[34,2,16,384]{3,2,1,0:T(8,128)(2,1)}, u32[]{:S(2)}, u32[]{:S(2)}) collective-permute-start(bf16[34,2,16,384]{3,2,1,0:T(8,128)(2,1)S(1)} %pad_maximum_fusion.3), channel_id=1, source_target_pairs={{4,8},{12,16},{20,24},{28,32},{36,40},{44,48},{52,56},{60,64},{68,... | collective-permute-start | bytes 2506760 | tf_op jit(solution)/shard_map/ppermute | solution.py:389
  11.3 2.3 %copy-start.6 = (bf16[512,2,384]{2,1,0:T(2,128)(2,1)S(1)}, bf16[512,2,384]{2,1,0:T(2,128)(2,1)}, u32[]{:S(2)}) copy-start(bf16[512,2,384]{2,1,0:T(2,128)(2,1)} %param.17) | copy-start | bytes 2359300
  11.5 2.2 %copy-start = (s32[512,1]{0,1:T(1,128)S(1)}, s32[512,1]{0,1:T(1,128)}, u32[]{:S(2)}) copy-start(s32[512,1]{0,1:T(1,128)} %param.18) | copy-start | bytes 6148
  11.5 2.2 %copy-start.1 = (s32[512]{0:T(512)S(1)}, s32[512]{0:T(512)}, u32[]{:S(2)}) copy-start(s32[512]{0:T(512)} %param.19) | copy-start | bytes 6148
  21.5 38.5 %all-to-all-start = ((bf16[32,208,128]{2,1,0:T(8,128)(2,1)}), bf16[32,208,128]{2,1,0:T(8,128)(2,1)S(1)}, u32[]{:S(2)}, u32[]{:S(2)}) async-start(bf16[32,208,128]{2,1,0:T(8,128)(2,1)} %wake_pack.1), calls=%async_computation | async-start | bytes 3407872 | tf_op jit(solution)/shard_map/all_to_all | solution.py:398
  31.8 23.0 %collective-permute-start = (bf16[9,2,64,384]{3,2,1,0:T(8,128)(2,1)}, bf16[9,2,64,384]{3,2,1,0:T(8,128)(2,1)S(1)}, u32[]{:S(2)}, u32[]{:S(2)}) collective-permute-start(bf16[9,2,64,384]{3,2,1,0:T(8,128)(2,1)} %pad_maximum_fusion), channel_id=1, source_target_pairs={{0,1},{1,2},{2,3},{4,5},{5,6},{6,7},{8,9},{9,10},{10,11},{12,13},{... | collective-permute-start | bytes 2654216 | tf_op jit(solution)/shard_map/ppermute | solution.py:26
  35.3 23.5 %collective-permute-start.1 = (bf16[9,2,64,384]{3,2,1,0:T(8,128)(2,1)}, bf16[9,2,64,384]{3,2,1,0:T(8,128)(2,1)S(1)}, u32[]{:S(2)}, u32[]{:S(2)}) collective-permute-start(bf16[9,2,64,384]{3,2,1,0:T(8,128)(2,1)} %pad_maximum_fusion.1), channel_id=1, source_target_pairs={{1,0},{2,1},{3,2},{5,4},{6,5},{7,6},{9,8},{10,9},{11,10},{13,12},{... | collective-permute-start | bytes 2654216 | tf_op jit(solution)/shard_map/ppermute | solution.py:26
  54.8 21.1 %copy-start.4 = (bf16[9,2,64,384]{3,2,1,0:T(8,128)(2,1)}, bf16[9,2,64,384]{3,2,1,0:T(8,128)(2,1)S(1)}, u32[]{:S(2)}) copy-start(bf16[9,2,64,384]{3,2,1,0:T(8,128)(2,1)S(1)} %collective-permute-done.refs_3_) | copy-start | bytes 2654212
  58.9 1.1 %copy-start.5 = (bf16[9,2,64,384]{3,2,1,0:T(8,128)(2,1)}, bf16[9,2,64,384]{3,2,1,0:T(8,128)(2,1)S(1)}, u32[]{:S(2)}) copy-start(bf16[9,2,64,384]{3,2,1,0:T(8,128)(2,1)S(1)} %collective-permute-done.1.refs_4_) | copy-start | bytes 2654212
  60.0 15.9 %collective-permute-start.6 = (bf16[16,2,16,384]{3,2,1,0:T(8,128)(2,1)}, bf16[16,2,16,384]{3,2,1,0:T(8,128)(2,1)}, u32[]{:S(2)}, u32[]{:S(2)}) collective-permute-start(bf16[16,2,16,384]{3,2,1,0:T(8,128)(2,1)} %pad_maximum_fusion.4), channel_id=1, source_target_pairs={{0,4},{4,0},{8,12},{12,8},{16,20},{20,16},{24,28},{28,24},{32,36},... | collective-permute-start | bytes 1179656 | tf_op jit(solution)/shard_map/ppermute | solution.py:411
  60.6 7.1 %collective-permute-start.4 = (bf16[2,64,384]{2,0,1:T(2,128)(2,1)S(1)}, bf16[2,64,384]{2,0,1:T(2,128)(2,1)S(1)}, u32[]{:S(2)}, u32[]{:S(2)}) collective-permute-start(bf16[2,64,384]{2,0,1:T(2,128)(2,1)S(1)} %copy.58), channel_id=1, source_target_pairs={{1,0},{2,3},{5,4},{6,7},{9,8},{10,11},{13,12},{14,15},{17,16},{18,... | collective-permute-start | bytes 294920 | tf_op jit(solution)/shard_map/ppermute | solution.py:418
  62.0 13.9 %collective-permute-start.7 = (bf16[16,2,16,384]{3,2,1,0:T(8,128)(2,1)S(1)}, bf16[16,2,16,384]{3,2,1,0:T(8,128)(2,1)S(1)}, u32[]{:S(2)}, u32[]{:S(2)}) collective-permute-start(bf16[16,2,16,384]{3,2,1,0:T(8,128)(2,1)S(1)} %pad_maximum_fusion.5), channel_id=1, source_target_pairs={{4,8},{12,16},{20,24},{28,32},{36,40},{44,48},{52,56},{60,64},{68,... | collective-permute-start | bytes 1179656 | tf_op jit(solution)/shard_map/ppermute | solution.py:412
  67.9 7.7 %collective-permute-start.5 = (bf16[2,64,384]{2,0,1:T(2,128)(2,1)S(1)}, bf16[2,64,384]{2,0,1:T(2,128)(2,1)S(1)}, u32[]{:S(2)}, u32[]{:S(2)}) collective-permute-start(bf16[2,64,384]{2,0,1:T(2,128)(2,1)S(1)} %fusion.12), channel_id=1, source_target_pairs={{0,3},{3,0},{4,7},{7,4},{8,11},{11,8},{12,15},{15,12},{16,19},{19,... | collective-permute-start | bytes 294920 | tf_op jit(solution)/shard_map/ppermute | solution.py:420
  75.9 0.8 copy-start.7
  95.5 1.7 %copy-start.3 = (bf16[32,64,2,384]{3,2,1,0:T(2,128)(2,1)}, bf16[32,64,2,384]{3,2,1,0:T(2,128)(2,1)S(1)}, u32[]{:S(2)}) copy-start(bf16[32,64,2,384]{3,2,1,0:T(2,128)(2,1)S(1)} %fusion.7) | copy-start | bytes 9437188
